TPU v7x, 512 devices: a whole 4x8x8 slice. The times are simulated.
512 devices in a mesh: tile: 64 (over z, x, core), tm: 8 (over y).
Axes of the slice: x: 4, y: 8, z: 8, core: 2. Of those that a mesh axis runs over, the one named last changes fastest.
Arguments:
- video_slabs: bfloat16 [64, 32, 96, 4, 128], P('tile', 'tm'), may hold values from -6 to 6
- slab_links: int32 [64, 4], P('tile'), may hold values from -1 to 63, as said below
- slab_extents: int32 [64, 2], P('tile'), may hold values from 1 to 128, as said below
- norm1_gain: float32 [96], replicated, may hold values from 0.1 to 1.9
- conv1_weight: bfloat16 [96, 2592], replicated, may hold values from -0.125 to 0.125
- conv1_bias: float32 [96], replicated, may hold values from -3 to 3
- norm2_gain: float32 [96], replicated, may hold values from 0.1 to 1.9
- conv2_weight: bfloat16 [96, 2592], replicated, may hold values from -0.125 to 0.125
- conv2_bias: float32 [96], replicated, may hold values from -3 to 3
- down_weight: bfloat16 [96, 864], replicated, may hold values from -0.21875 to 0.21875
- down_bias: float32 [96], replicated, may hold values from -3 to 3
Outputs:
- encoded: bfloat16 [64, 32, 96, 128], P('tile', 'tm')
Inputs may be any that keep to these rules, and one draw needn't show every extreme that they name: `slab_links`: row s holds the links of slab s on a canvas grid of 8 slabs a row, in the order up, down, left, right: s - 8, s + 8, s - 1 and s + 1, or -1 at the border of its clip. Linked slabs form whole rectangular clips: links are mutual, and the left link of the up link is the up link of the left link, likewise at every corner. `slab_extents`: row s holds the rows and the columns of slab s that lie inside its clip, counted from its top left corner; a slab with a down link has all 4 rows inside, one with a right link all 128 columns.
All inputs are finite; a program needn't handle non-finite values.
Results may differ from a plain program's by a relative error of at most 0.0052.
Values may be sent and summed in bfloat16 or wider, within the bound.
A program may use at most 64 MiB of HBM per device.

v0:
```python
import jax
import jax.numpy as jnp
from jax import lax
from jax.sharding import PartitionSpec as P

GRID_COLUMN_COUNT = 8


norm_eps = 1e-06


def passed_along(block, axis, distance):
    devices = range(lax.axis_size(axis))
    route = [(i - distance, i) for i in devices if i - distance in devices]
    return lax.ppermute(block, axis, route)


def activate(values, scale_gain, inside):
    widened = values.astype(jnp.float32)
    mean_square = jnp.mean(widened * widened, axis=1, keepdims=True)
    normed = widened * lax.rsqrt(mean_square + norm_eps) * scale_gain[None, :, None, None]
    return (jax.nn.silu(normed) * inside).astype(jnp.bfloat16)


def from_above(edge_rows):
    return passed_along(edge_rows, "tile", GRID_COLUMN_COUNT)


def from_below(edge_rows):
    return passed_along(edge_rows, "tile", -GRID_COLUMN_COUNT)


def from_left(edge_cols):
    return passed_along(edge_cols, "tile", 1)


def from_right(edge_cols):
    return passed_along(edge_cols, "tile", -1)


def earlier(frames_sent):
    return passed_along(frames_sent, "tm", 1)


def with_rims(stacked, link_ok):
    frame_depth, channels, slab_rows, slab_cols = stacked.shape
    upper_row = from_above(stacked[:, :, slab_rows - 1, :]) * link_ok[0]
    lower_row = from_below(stacked[:, :, 0, :]) * link_ok[1]
    taller = jnp.concatenate([upper_row[:, :, None, :], stacked, lower_row[:, :, None, :]], axis=2)
    left_edge = (
        from_left(taller[:, :, :, slab_cols - 1].reshape(-1)).reshape(
            frame_depth, channels, slab_rows + 2
        )
        * link_ok[2]
    )
    right_edge = (
        from_right(taller[:, :, :, 0].reshape(-1)).reshape(frame_depth, channels, slab_rows + 2)
        * link_ok[3]
    )
    return (taller, left_edge, right_edge)


def window_conv(taller, left_edge, right_edge, weight):
    frame_depth, channels, tall_rows, slab_cols = taller.shape
    frame_count = frame_depth - 2
    slab_rows = tall_rows - 2
    filter_weight = (
        weight.reshape(channels, 3, 3, 3, channels)
        .transpose(1, 2, 3, 0, 4)
        .reshape(9, 3, channels, channels)
    )
    window_patches = jnp.stack(
        [
            taller[dt : dt + frame_count, :, dr : dr + slab_rows, :]
            for dt in range(3)
            for dr in range(3)
        ]
    )
    edge_left = jnp.stack(
        [
            left_edge[dt : dt + frame_count, :, dr : dr + slab_rows]
            for dt in range(3)
            for dr in range(3)
        ]
    )
    edge_right = jnp.stack(
        [
            right_edge[dt : dt + frame_count, :, dr : dr + slab_rows]
            for dt in range(3)
            for dr in range(3)
        ]
    )
    column_span = jnp.einsum(
        "eqim,exmpl->qxipl", filter_weight, window_patches, preferred_element_type=jnp.float32
    )
    left_term = jnp.einsum(
        "goc,gtcr->tor", filter_weight[:, 0], edge_left, preferred_element_type=jnp.float32
    )
    right_term = jnp.einsum(
        "goc,gtcr->tor", filter_weight[:, 2], edge_right, preferred_element_type=jnp.float32
    )
    from_west = jnp.concatenate(
        [left_term[..., None], column_span[0][..., : slab_cols - 1]], axis=-1
    )
    eastern_neighbour = jnp.concatenate([column_span[2][..., 1:], right_term[..., None]], axis=-1)
    return column_span[1] + from_west + eastern_neighbour


def down_conv(taller, right_edge, weight):
    frame_count, channels, tall_rows, slab_cols = taller.shape
    half_cols = slab_cols // 2
    half_rows = (tall_rows - 1) // 2
    filter_weight = (
        weight.reshape(channels, 3, 3, channels)
        .transpose(1, 2, 0, 3)
        .reshape(9, channels, channels)
    )
    source_col = jnp.arange(slab_cols, dtype=jnp.int32)[:, None]
    target_col = jnp.arange(half_cols, dtype=jnp.int32)[None, :]
    last_col = jnp.arange(half_cols, dtype=jnp.int32) == half_cols - 1
    picked = []
    for dc in range(3):
        select_mask = (source_col == 2 * target_col + dc).astype(jnp.bfloat16)
        chosen = jnp.einsum(
            "tcrw,wj->tcrj", taller, select_mask, preferred_element_type=jnp.float32
        ).astype(jnp.bfloat16)
        if dc == 2:
            chosen = jnp.where(last_col[None, None, None, :], right_edge[..., None], chosen)
        picked.append(chosen)
    window_patches = jnp.stack(
        [picked[dc][:, :, dr : dr + 2 * half_rows - 1 : 2, :] for dr in range(3) for dc in range(3)]
    )
    return jnp.einsum(
        "goc,gtcij->toij", filter_weight, window_patches, preferred_element_type=jnp.float32
    )


def per_device(
    video_slabs,
    slab_links,
    slab_extents,
    norm1_gain,
    conv1_weight,
    conv1_bias,
    norm2_gain,
    conv2_weight,
    conv2_bias,
    down_weight,
    down_bias,
):
    frames_in = video_slabs[0]
    frame_count, channels, slab_rows, slab_cols = frames_in.shape
    links_here = slab_links[0]
    row_ok = jnp.arange(slab_rows, dtype=jnp.int32) < slab_extents[0, 0]
    col_ok = jnp.arange(slab_cols, dtype=jnp.int32) < slab_extents[0, 1]
    inside = (row_ok[:, None] & col_ok[None, :]).astype(jnp.float32)
    link_ok = (links_here >= 0).astype(jnp.bfloat16)
    first_bias = conv1_bias[None, :, None, None]
    history = earlier(frames_in[frame_count - 2 :])
    first_act = activate(jnp.concatenate([history, frames_in], axis=0), norm1_gain, inside)
    convolved_output = window_conv(*with_rims(first_act, link_ok), conv1_weight) + first_bias
    current_act = activate(convolved_output, norm2_gain, inside)
    second_act = jnp.concatenate([earlier(current_act[frame_count - 2 :]), current_act], axis=0)
    convolved_output = (
        window_conv(*with_rims(second_act, link_ok), conv2_weight) + conv2_bias[None, :, None, None]
    )
    block_result = ((frames_in.astype(jnp.float32) + convolved_output) * inside).astype(
        jnp.bfloat16
    )
    lower_row = from_below(block_result[:, :, 0, :]) * link_ok[1]
    taller = jnp.concatenate([block_result, lower_row[:, :, None, :]], axis=2)
    right_edge = (
        from_right(taller[:, :, :, 0].reshape(-1)).reshape(frame_count, channels, slab_rows + 1)
        * link_ok[3]
    )
    reduced = down_conv(taller, right_edge, down_weight) + down_bias[None, :, None, None]
    half_rows = jnp.arange(slab_rows // 2, dtype=jnp.int32)
    half_cols = jnp.arange(slab_cols // 2, dtype=jnp.int32)
    out_rows = (2 * half_rows + 2 <= slab_extents[0, 0]) | (links_here[1] >= 0)
    out_cols = (2 * half_cols + 2 <= slab_extents[0, 1]) | (links_here[3] >= 0)
    out_keep = (out_rows[:, None] & out_cols[None, :]).astype(jnp.float32)
    masked = reduced * out_keep
    return masked.astype(jnp.bfloat16).reshape(frame_count, channels, -1)[None]


def solution(mesh):
    placed = (
        P("tile", "tm", None, None, None),
        P("tile", None),
        P("tile", None),
        P(),
        P(),
        P(),
        P(),
        P(),
        P(),
        P(),
        P(),
    )
    return jax.shard_map(
        per_device,
        mesh=mesh,
        in_specs=placed,
        out_specs=P("tile", "tm", None, None),
        check_vma=False,
    )
```

profile of v0, /device:TPU:223, one launch (start us, length us, event | category | flops | bytes accessed | tf_op | source)
XLA Modules:
  0.0 174.1 jit_solution(2145304677453215925)
XLA Ops:
  1.1 4.4 %collective-permute-start = (bf16[2,96,4,128]{3,1,0,2:T(8,128)(2,1)S(1)}, bf16[2,96,4,128]{3,1,0,2:T(8,128)(2,1)S(1)}, u32[]{:S(2)}, u32[]{:S(2)}) collective-permute-start(bf16[2,96,4,128]{3,1,0,2:T(8,128)(2,1)S(1)} %slice_bitcast_fusion.22), channel_id=1, source_target_pairs={{0,1},{1,2},{2,3},{3,4},{4,5},{5,6},{6,7},{8,9},{9,10},{10,11},{11... | collective-permute-start | bytes 589832 | tf_op jit(solution)/shard_map/ppermute | solution.py:15
  13.9 5.2 %collective-permute-start.1 = (bf16[6,96,128]{2,1,0:T(8,128)(2,1)S(1)}, bf16[6,96,128]{2,1,0:T(8,128)(2,1)S(1)}, u32[]{:S(2)}, u32[]{:S(2)}) collective-permute-start(bf16[6,96,128]{2,1,0:T(8,128)(2,1)S(1)} %get-tuple-element.29), channel_id=1, source_target_pairs={{0,64},{8,72},{16,80},{24,88},{32,96},{40,104},{48,112},{56,120},{... | collective-permute-start | bytes 442376 | tf_op jit(solution)/shard_map/ppermute | solution.py:15
  22.5 1.9 %collective-permute-start.2 = (bf16[6,96,128]{2,1,0:T(8,128)(2,1)S(1)}, bf16[6,96,128]{2,1,0:T(8,128)(2,1)S(1)}, u32[]{:S(2)}, u32[]{:S(2)}) collective-permute-start(bf16[6,96,128]{2,1,0:T(8,128)(2,1)S(1)} %get-tuple-element.30), channel_id=1, source_target_pairs={{64,0},{72,8},{80,16},{88,24},{96,32},{104,40},{112,48},{120,56},{... | collective-permute-start | bytes 442376 | tf_op jit(solution)/shard_map/ppermute | solution.py:15
  26.5 3.0 %collective-permute-done.2 = bf16[6,96,128]{2,1,0:T(8,128)(2,1)S(1)} collective-permute-done((bf16[6,96,128]{2,1,0:T(8,128)(2,1)S(1)}, bf16[6,96,128]{2,1,0:T(8,128)(2,1)S(1)}, u32[]{:S(2)}, u32[]{:S(2)}) %collective-permute-start.2) | collective-permute-done | bytes 147488 | tf_op jit(solution)/shard_map/ppermute | solution.py:15
  30.8 3.5 %copy.248 = bf16[6,96,6,1]{2,1,0,3:T(8,128)(2,1)S(1)} copy(bf16[6,96,6,1]{3,1,0,2:T(8,128)(2,1)S(1)} %get-tuple-element.14) | data formatting | bytes 13824 | tf_op jit(solution)/shard_map/slice | solution.py:57
  34.5 4.3 %collective-permute-start.4 = (bf16[3456]{0:T(1024)(128)(2,1)S(1)}, bf16[3456]{0:T(1024)(128)(2,1)S(1)}, u32[]{:S(2)}, u32[]{:S(2)}) collective-permute-start(bf16[3456]{0:T(1024)(128)(2,1)S(1)} %reshape_squeeze.16), channel_id=1, source_target_pairs={{8,0},{16,8},{24,16},{32,24},{40,32},{48,40},{56,48},{64,56},{72,6... | collective-permute-start | bytes 20744 | tf_op jit(solution)/shard_map/ppermute | solution.py:15
  42.4 1.4 fusion.7
  45.1 3.5 %copy.237 = bf16[6,96,6,1]{2,1,0,3:T(8,128)(2,1)S(1)} copy(bf16[6,96,6,1]{3,1,0,2:T(8,128)(2,1)S(1)} %get-tuple-element.13) | data formatting | bytes 13824 | tf_op jit(solution)/shard_map/slice | solution.py:51
  48.8 4.8 %collective-permute-start.3 = (bf16[3456]{0:T(1024)(128)(2,1)S(1)}, bf16[3456]{0:T(1024)(128)(2,1)S(1)}, u32[]{:S(2)}, u32[]{:S(2)}) collective-permute-start(bf16[3456]{0:T(1024)(128)(2,1)S(1)} %reshape_squeeze.15), channel_id=1, source_target_pairs={{0,8},{8,16},{16,24},{24,32},{32,40},{40,48},{48,56},{56,64},{64,7... | collective-permute-start | bytes 20744 | tf_op jit(solution)/shard_map/ppermute | solution.py:15
  53.6 3.2 %slice_bitcast_fusion.26 = (f32[1,4,96,4,127]{4,2,1,3,0:T(8,128)}, f32[4,96,4,127]{3,1,0,2:T(8,128)S(1)}, f32[4,96,4,127]{3,1,0,2:T(8,128)}, f32[1,4,96,4,127]{4,2,1,3,0:T(8,128)}) fusion(f32[4,96,4,128]{3,1,0,2:T(8,128)} %get-tuple-element.10, f32[4,96,4,128]{3,1,0,2:T(8,128)} %get-tuple-element.9), kind=kLoop, calls=%fused_computation.210 | loop fusion | bytes 4681728 | tf_op jit(solution)/shard_map/concatenate | solution.py:105
  80.0 2.2 %multiply_reduce_fusion = (f32[4,4,128]{2,0,1:T(4,128)S(1)}, f32[4,96,4,128]{3,1,0,2:T(8,128)S(1)}) fusion(f32[96]{0:T(128)S(1)} %copy-done.13, f32[4,96,4,1]{3,1,0,2:T(8,128)} %copy.258, f32[4,96,4,127]{3,1,0,2:T(8,128)S(1)} %get-tuple-element.18, f32[4,96,4,127]{3,1,0,2:T(8,128)} %get-tuple-element.79, f32[4,96,4,1]{3,1,0,2:T(8,128)} %copy.247, ...), kind=kLoop, calls=%fused_computation.54 | loop fusion | flops 1374208 | bytes 3154304 | tf_op jit(solution)/shard_map/reduce_sum | solution.py:20
  82.5 2.3 %collective-permute-start.5 = (bf16[2,96,4,128]{3,1,0,2:T(8,128)(2,1)S(1)}, bf16[2,96,4,128]{3,1,0,2:T(8,128)(2,1)S(1)}, u32[]{:S(2)}, u32[]{:S(2)}) collective-permute-start(bf16[2,96,4,128]{3,1,0,2:T(8,128)(2,1)S(1)} %slice.455), channel_id=1, source_target_pairs={{0,1},{1,2},{2,3},{3,4},{4,5},{5,6},{6,7},{8,9},{9,10},{10,11},{11... | collective-permute-start | bytes 589832 | tf_op jit(solution)/shard_map/ppermute | solution.py:15
  84.9 4.4 %collective-permute-done.5 = bf16[2,96,4,128]{3,1,0,2:T(8,128)(2,1)S(1)} collective-permute-done((bf16[2,96,4,128]{3,1,0,2:T(8,128)(2,1)S(1)}, bf16[2,96,4,128]{3,1,0,2:T(8,128)(2,1)S(1)}, u32[]{:S(2)}, u32[]{:S(2)}) %collective-permute-start.5) | collective-permute-done | bytes 196640 | tf_op jit(solution)/shard_map/ppermute | solution.py:15
  89.4 1.9 %collective-permute-start.7 = (bf16[6,96,128]{2,1,0:T(8,128)(2,1)S(1)}, bf16[6,96,128]{2,1,0:T(8,128)(2,1)}, u32[]{:S(2)}, u32[]{:S(2)}) collective-permute-start(bf16[6,96,128]{2,1,0:T(8,128)(2,1)S(1)} %get-tuple-element.24), channel_id=1, source_target_pairs={{64,0},{72,8},{80,16},{88,24},{96,32},{104,40},{112,48},{120,56},{... | collective-permute-start | bytes 442376 | tf_op jit(solution)/shard_map/ppermute | solution.py:15
  92.7 2.1 %copy.261 = bf16[96,2592]{0,1:T(8,128)(2,1)} copy(bf16[96,2592]{1,0:T(8,128)(2,1)} %param.18) | data formatting | bytes 995328 | tf_op args[7]
  94.8 2.2 %copy.262 = bf16[3,3,3,96,96]{4,3,1,0,2:T(8,128)(2,1)} copy(bf16[3,3,3,96,96]{3,4,2,1,0:T(8,128)(2,1)} %bitcast.365) | data formatting | bytes 995328 | tf_op jit(solution)/shard_map/transpose | solution.py:69
  100.0 4.6 %collective-permute-start.6 = (bf16[6,96,128]{2,1,0:T(8,128)(2,1)S(1)}, bf16[6,96,128]{2,1,0:T(8,128)(2,1)S(1)}, u32[]{:S(2)}, u32[]{:S(2)}) collective-permute-start(bf16[6,96,128]{2,1,0:T(8,128)(2,1)S(1)} %get-tuple-element.25), channel_id=1, source_target_pairs={{0,64},{8,72},{16,80},{24,88},{32,96},{40,104},{48,112},{56,120},{... | collective-permute-start | bytes 442376 | tf_op jit(solution)/shard_map/ppermute | solution.py:15
  104.5 1.6 multiply_bitcast_fusion
  106.2 1.7 collective-permute-done.6
  113.1 3.5 %copy.265 = bf16[6,96,6,1]{2,1,0,3:T(8,128)(2,1)S(1)} copy(bf16[6,96,6,1]{3,1,0,2:T(8,128)(2,1)S(1)} %get-tuple-element.12) | data formatting | bytes 13824 | tf_op jit(solution)/shard_map/slice | solution.py:51
  116.8 6.2 %collective-permute-start.8 = (bf16[3456]{0:T(1024)(128)(2,1)S(1)}, bf16[3456]{0:T(1024)(128)(2,1)S(1)}, u32[]{:S(2)}, u32[]{:S(2)}) collective-permute-start(bf16[3456]{0:T(1024)(128)(2,1)S(1)} %reshape_squeeze.17), channel_id=1, source_target_pairs={{0,8},{8,16},{16,24},{24,32},{32,40},{40,48},{48,56},{56,64},{64,7... | collective-permute-start | bytes 20744 | tf_op jit(solution)/shard_map/ppermute | solution.py:15
  123.0 3.6 %fusion.4 = f32[3,4,96,4,128]{4,2,1,3,0:T(8,128)S(1)} fusion(bf16[9,3,96,96,1,1]{3,2,4,5,0,1:T(8,128)(2,1)} %bitcast.369, bf16[9,4,96,4,128]{4,2,1,3,0:T(8,128)(2,1)} %copy-done.12), kind=kOutput, calls=%fused_computation.4 | convolution fusion | flops 1019215872 | bytes 6395904 | tf_op jit(solution)/shard_map/eqim,exmpl->qxipl/dot_general | solution.py:93
  128.2 3.5 %copy.276 = bf16[6,96,6,1]{2,1,0,3:T(8,128)(2,1)S(1)} copy(bf16[6,96,6,1]{3,1,0,2:T(8,128)(2,1)S(1)} %get-tuple-element.11) | data formatting | bytes 13824 | tf_op jit(solution)/shard_map/slice | solution.py:57
  131.9 1.9 %collective-permute-start.9 = (bf16[3456]{0:T(1024)(128)(2,1)S(1)}, bf16[3456]{0:T(1024)(128)(2,1)S(1)}, u32[]{:S(2)}, u32[]{:S(2)}) collective-permute-start(bf16[3456]{0:T(1024)(128)(2,1)S(1)} %reshape_squeeze.18), channel_id=1, source_target_pairs={{8,0},{16,8},{24,16},{32,24},{40,32},{48,40},{56,48},{64,56},{72,6... | collective-permute-start | bytes 20744 | tf_op jit(solution)/shard_map/ppermute | solution.py:15
  137.8 2.3 %collective-permute-done.9 = bf16[3456]{0:T(1024)(128)(2,1)S(1)} collective-permute-done((bf16[3456]{0:T(1024)(128)(2,1)S(1)}, bf16[3456]{0:T(1024)(128)(2,1)S(1)}, u32[]{:S(2)}, u32[]{:S(2)}) %collective-permute-start.9) | collective-permute-done | bytes 6944 | tf_op jit(solution)/shard_map/ppermute | solution.py:15
  143.9 1.7 fusion.26
  145.7 1.9 %collective-permute-start.10 = (bf16[4,96,128]{2,1,0:T(8,128)(2,1)S(1)}, bf16[4,96,128]{2,1,0:T(8,128)(2,1)S(1)}, u32[]{:S(2)}, u32[]{:S(2)}) collective-permute-start(bf16[4,96,128]{2,1,0:T(8,128)(2,1)S(1)} %slice_bitcast_fusion.25), channel_id=1, source_target_pairs={{64,0},{72,8},{80,16},{88,24},{96,32},{104,40},{112,48},{120,56},{... | collective-permute-start | bytes 294920 | tf_op jit(solution)/shard_map/ppermute | solution.py:15
  147.6 4.6 %collective-permute-done.10 = bf16[4,96,128]{2,1,0:T(8,128)(2,1)S(1)} collective-permute-done((bf16[4,96,128]{2,1,0:T(8,128)(2,1)S(1)}, bf16[4,96,128]{2,1,0:T(8,128)(2,1)S(1)}, u32[]{:S(2)}, u32[]{:S(2)}) %collective-permute-start.10) | collective-permute-done | bytes 98336 | tf_op jit(solution)/shard_map/ppermute | solution.py:15
  154.7 2.4 %copy.289 = bf16[4,96,5,1]{2,1,0,3:T(8,128)(2,1)S(1)} copy(bf16[4,96,5,1]{3,1,0,2:T(8,128)(2,1)S(1)} %fusion.33) | data formatting | bytes 7680 | tf_op jit(solution)/shard_map/slice | solution.py:173
  157.3 1.9 %collective-permute-start.11 = (bf16[1920]{0:T(1024)(128)(2,1)S(1)}, bf16[1920]{0:T(1024)(128)(2,1)S(1)}, u32[]{:S(2)}, u32[]{:S(2)}) collective-permute-start(bf16[1920]{0:T(1024)(128)(2,1)S(1)} %reshape_squeeze.19), channel_id=1, source_target_pairs={{8,0},{16,8},{24,16},{32,24},{40,32},{48,40},{56,48},{64,56},{72,6... | collective-permute-start | bytes 11528 | tf_op jit(solution)/shard_map/ppermute | solution.py:15
  159.9 5.7 %collective-permute-done.11 = bf16[1920]{0:T(1024)(128)(2,1)S(1)} collective-permute-done((bf16[1920]{0:T(1024)(128)(2,1)S(1)}, bf16[1920]{0:T(1024)(128)(2,1)S(1)}, u32[]{:S(2)}, u32[]{:S(2)}) %collective-permute-start.11) | collective-permute-done | bytes 3872 | tf_op jit(solution)/shard_map/ppermute | solution.py:15
  171.5 1.7 fusion.19
  (224 shorter events, 72.8 us)
Async XLA Ops:
  0.0 20.4 %copy-start.9 = (bf16[96,2592]{1,0:T(8,128)(2,1)S(1)}, bf16[96,2592]{1,0:T(8,128)(2,1)}, u32[]{:S(2)}) copy-start(bf16[96,2592]{1,0:T(8,128)(2,1)} %param.15) | copy-start | bytes 1492996
  1.1 11.5 %collective-permute-start = (bf16[2,96,4,128]{3,1,0,2:T(8,128)(2,1)S(1)}, bf16[2,96,4,128]{3,1,0,2:T(8,128)(2,1)S(1)}, u32[]{:S(2)}, u32[]{:S(2)}) collective-permute-start(bf16[2,96,4,128]{3,1,0,2:T(8,128)(2,1)S(1)} %slice_bitcast_fusion.22), channel_id=1, source_target_pairs={{0,1},{1,2},{2,3},{3,4},{4,5},{5,6},{6,7},{8,9},{9,10},{10,11},{11... | collective-permute-start | bytes 589832 | tf_op jit(solution)/shard_map/ppermute | solution.py:15
  13.9 10.5 %collective-permute-start.1 = (bf16[6,96,128]{2,1,0:T(8,128)(2,1)S(1)}, bf16[6,96,128]{2,1,0:T(8,128)(2,1)S(1)}, u32[]{:S(2)}, u32[]{:S(2)}) collective-permute-start(bf16[6,96,128]{2,1,0:T(8,128)(2,1)S(1)} %get-tuple-element.29), channel_id=1, source_target_pairs={{0,64},{8,72},{16,80},{24,88},{32,96},{40,104},{48,112},{56,120},{... | collective-permute-start | bytes 442376 | tf_op jit(solution)/shard_map/ppermute | solution.py:15
  22.5 7.1 %collective-permute-start.2 = (bf16[6,96,128]{2,1,0:T(8,128)(2,1)S(1)}, bf16[6,96,128]{2,1,0:T(8,128)(2,1)S(1)}, u32[]{:S(2)}, u32[]{:S(2)}) collective-permute-start(bf16[6,96,128]{2,1,0:T(8,128)(2,1)S(1)} %get-tuple-element.30), channel_id=1, source_target_pairs={{64,0},{72,8},{80,16},{88,24},{96,32},{104,40},{112,48},{120,56},{... | collective-permute-start | bytes 442376 | tf_op jit(solution)/shard_map/ppermute | solution.py:15
  30.8 11.4 %copy-start.6 = (bf16[1,4,96,4,128]{4,2,1,3,0:T(8,128)(2,1)S(1)}, bf16[1,4,96,4,128]{4,2,1,3,0:T(8,128)(2,1)}, u32[]{:S(2)}) copy-start(bf16[1,4,96,4,128]{4,2,1,3,0:T(8,128)(2,1)} %get-tuple-element.19) | copy-start | bytes 1179652
  30.8 11.5 %copy-start.5 = (bf16[1,4,96,4,128]{4,2,1,3,0:T(8,128)(2,1)S(1)}, bf16[1,4,96,4,128]{4,2,1,3,0:T(8,128)(2,1)}, u32[]{:S(2)}) copy-start(bf16[1,4,96,4,128]{4,2,1,3,0:T(8,128)(2,1)} %get-tuple-element.26) | copy-start | bytes 1179652
  34.3 7.8 %copy-start.7 = (bf16[1,4,96,4,128]{4,2,1,3,0:T(8,128)(2,1)S(1)}, bf16[1,4,96,4,128]{4,2,1,3,0:T(8,128)(2,1)}, u32[]{:S(2)}) copy-start(bf16[1,4,96,4,128]{4,2,1,3,0:T(8,128)(2,1)} %get-tuple-element.27) | copy-start | bytes 1179652
  34.5 22.3 %collective-permute-start.4 = (bf16[3456]{0:T(1024)(128)(2,1)S(1)}, bf16[3456]{0:T(1024)(128)(2,1)S(1)}, u32[]{:S(2)}, u32[]{:S(2)}) collective-permute-start(bf16[3456]{0:T(1024)(128)(2,1)S(1)} %reshape_squeeze.16), channel_id=1, source_target_pairs={{8,0},{16,8},{24,16},{32,24},{40,32},{48,40},{56,48},{64,56},{72,6... | collective-permute-start | bytes 20744 | tf_op jit(solution)/shard_map/ppermute | solution.py:15
  39.8 2.6 %copy-start.8 = (bf16[3,3,3,96,96]{4,3,1,0,2:T(8,128)(2,1)S(1)}, bf16[3,3,3,96,96]{4,3,1,0,2:T(8,128)(2,1)}, u32[]{:S(2)}) copy-start(bf16[3,3,3,96,96]{4,3,1,0,2:T(8,128)(2,1)} %copy.234) | copy-start | bytes 1492996
  48.8 19.6 %collective-permute-start.3 = (bf16[3456]{0:T(1024)(128)(2,1)S(1)}, bf16[3456]{0:T(1024)(128)(2,1)S(1)}, u32[]{:S(2)}, u32[]{:S(2)}) collective-permute-start(bf16[3456]{0:T(1024)(128)(2,1)S(1)} %reshape_squeeze.15), channel_id=1, source_target_pairs={{0,8},{8,16},{16,24},{24,32},{32,40},{40,48},{48,56},{56,64},{64,7... | collective-permute-start | bytes 20744 | tf_op jit(solution)/shard_map/ppermute | solution.py:15
  57.6 22.4 %copy-start.13 = (f32[96]{0:T(128)S(1)}, f32[96]{0:T(128)}, u32[]{:S(2)}) copy-start(f32[96]{0:T(128)} %param.16) | copy-start | bytes 1156
  70.3 11.9 %copy-start.14 = (f32[96]{0:T(128)S(1)}, f32[96]{0:T(128)}, u32[]{:S(2)}) copy-start(f32[96]{0:T(128)} %param.17) | copy-start | bytes 1156
  78.8 6.1 %copy-start.17 = (pred[2]{0:T(512)(128)(4,1)S(1)}, pred[2]{0:T(512)(128)(4,1)}, u32[]{:S(2)}) copy-start(pred[2]{0:T(512)(128)(4,1)} %compare_or_fusion.1) | copy-start | bytes 10
  80.0 11.8 %copy-start.11 = (bf16[96,864]{1,0:T(8,128)(2,1)S(1)}, bf16[96,864]{1,0:T(8,128)(2,1)}, u32[]{:S(2)}) copy-start(bf16[96,864]{1,0:T(8,128)(2,1)} %param.20) | copy-start | bytes 497668
  82.5 6.8 %collective-permute-start.5 = (bf16[2,96,4,128]{3,1,0,2:T(8,128)(2,1)S(1)}, bf16[2,96,4,128]{3,1,0,2:T(8,128)(2,1)S(1)}, u32[]{:S(2)}, u32[]{:S(2)}) collective-permute-start(bf16[2,96,4,128]{3,1,0,2:T(8,128)(2,1)S(1)} %slice.455), channel_id=1, source_target_pairs={{0,1},{1,2},{2,3},{3,4},{4,5},{5,6},{6,7},{8,9},{9,10},{10,11},{11... | collective-permute-start | bytes 589832 | tf_op jit(solution)/shard_map/ppermute | solution.py:15
  89.4 15.2 %collective-permute-start.7 = (bf16[6,96,128]{2,1,0:T(8,128)(2,1)S(1)}, bf16[6,96,128]{2,1,0:T(8,128)(2,1)}, u32[]{:S(2)}, u32[]{:S(2)}) collective-permute-start(bf16[6,96,128]{2,1,0:T(8,128)(2,1)S(1)} %get-tuple-element.24), channel_id=1, source_target_pairs={{64,0},{72,8},{80,16},{88,24},{96,32},{104,40},{112,48},{120,56},{... | collective-permute-start | bytes 442376 | tf_op jit(solution)/shard_map/ppermute | solution.py:15
  100.0 7.9 %collective-permute-start.6 = (bf16[6,96,128]{2,1,0:T(8,128)(2,1)S(1)}, bf16[6,96,128]{2,1,0:T(8,128)(2,1)S(1)}, u32[]{:S(2)}, u32[]{:S(2)}) collective-permute-start(bf16[6,96,128]{2,1,0:T(8,128)(2,1)S(1)} %get-tuple-element.25), channel_id=1, source_target_pairs={{0,64},{8,72},{16,80},{24,88},{32,96},{40,104},{48,112},{56,120},{... | collective-permute-start | bytes 442376 | tf_op jit(solution)/shard_map/ppermute | solution.py:15
  108.7 1.4 copy-start.1
  108.7 1.6 copy-start.2
  108.7 1.8 %copy-start.3 = (f32[1,4,96,4,1]{4,2,1,3,0:T(8,128)S(1)}, f32[1,4,96,4,1]{4,2,1,3,0:T(8,128)}, u32[]{:S(2)}) copy-start(f32[1,4,96,4,1]{4,2,1,3,0:T(8,128)} %copy.259) | copy-start | bytes 18436
  111.3 1.7 copy-start.12
  116.8 17.3 %collective-permute-start.8 = (bf16[3456]{0:T(1024)(128)(2,1)S(1)}, bf16[3456]{0:T(1024)(128)(2,1)S(1)}, u32[]{:S(2)}, u32[]{:S(2)}) collective-permute-start(bf16[3456]{0:T(1024)(128)(2,1)S(1)} %reshape_squeeze.17), channel_id=1, source_target_pairs={{0,8},{8,16},{16,24},{24,32},{32,40},{40,48},{48,56},{56,64},{64,7... | collective-permute-start | bytes 20744 | tf_op jit(solution)/shard_map/ppermute | solution.py:15
  126.6 1.4 copy-start.4
  131.9 8.3 %collective-permute-start.9 = (bf16[3456]{0:T(1024)(128)(2,1)S(1)}, bf16[3456]{0:T(1024)(128)(2,1)S(1)}, u32[]{:S(2)}, u32[]{:S(2)}) collective-permute-start(bf16[3456]{0:T(1024)(128)(2,1)S(1)} %reshape_squeeze.18), channel_id=1, source_target_pairs={{8,0},{16,8},{24,16},{32,24},{40,32},{48,40},{56,48},{64,56},{72,6... | collective-permute-start | bytes 20744 | tf_op jit(solution)/shard_map/ppermute | solution.py:15
  134.9 9.0 %copy-start.15 = (f32[96]{0:T(128)S(1)}, f32[96]{0:T(128)}, u32[]{:S(2)}) copy-start(f32[96]{0:T(128)} %param.19) | copy-start | bytes 1156
  142.4 10.6 %copy-start.18 = (s32[64]{0:T(128)S(1)}, s32[64]{0:T(128)}, u32[]{:S(2)}) copy-start(s32[64]{0:T(128)} %iota_multiply_fusion) | copy-start | bytes 772
  143.9 10.3 %copy-start.20 = (s32[64]{0:T(128)S(1)}, s32[64]{0:T(128)}, u32[]{:S(2)}) copy-start(s32[64]{0:T(128)} %broadcast_add_fusion) | copy-start | bytes 772
  145.7 20.8 %copy-start.19 = (pred[64]{0:T(512)(128)(4,1)S(1)}, pred[64]{0:T(512)(128)(4,1)}, u32[]{:S(2)}) copy-start(pred[64]{0:T(512)(128)(4,1)} %iota_compare_fusion.3) | copy-start | bytes 196
  145.7 6.6 %collective-permute-start.10 = (bf16[4,96,128]{2,1,0:T(8,128)(2,1)S(1)}, bf16[4,96,128]{2,1,0:T(8,128)(2,1)S(1)}, u32[]{:S(2)}, u32[]{:S(2)}) collective-permute-start(bf16[4,96,128]{2,1,0:T(8,128)(2,1)S(1)} %slice_bitcast_fusion.25), channel_id=1, source_target_pairs={{64,0},{72,8},{80,16},{88,24},{96,32},{104,40},{112,48},{120,56},{... | collective-permute-start | bytes 294920 | tf_op jit(solution)/shard_map/ppermute | solution.py:15
  153.1 18.5 %copy-start.10 = (bf16[96,864]{0,1:T(8,128)(2,1)S(1)}, bf16[96,864]{0,1:T(8,128)(2,1)}, u32[]{:S(2)}) copy-start(bf16[96,864]{0,1:T(8,128)(2,1)} %copy.292) | copy-start | bytes 497668
  154.2 19.1 %copy-start.16 = (f32[96]{0:T(128)S(1)}, f32[96]{0:T(128)}, u32[]{:S(2)}) copy-start(f32[96]{0:T(128)} %param.21) | copy-start | bytes 1156
  157.3 8.2 %collective-permute-start.11 = (bf16[1920]{0:T(1024)(128)(2,1)S(1)}, bf16[1920]{0:T(1024)(128)(2,1)S(1)}, u32[]{:S(2)}, u32[]{:S(2)}) collective-permute-start(bf16[1920]{0:T(1024)(128)(2,1)S(1)} %reshape_squeeze.19), channel_id=1, source_target_pairs={{8,0},{16,8},{24,16},{32,24},{40,32},{48,40},{56,48},{64,56},{72,6... | collective-permute-start | bytes 11528 | tf_op jit(solution)/shard_map/ppermute | solution.py:15
  (1 other events, 1.1 us)
where the time goes:
time: 176 us; the launch traced here: 174 us
  local copies, waits for them, and re-layouts  74.8 us (42%)
  starting transfers between devices  41.4 us (24%)
  waiting for transfers between devices  21.7 us (12%)
  other arithmetic  21.2 us (12%)
  matrix products  12.7 us (7%)
  between operations  2.28 us (1%)
    ppermute x12, starting transfers between devices, passed_along(): return lax.ppermute(block, axis, route)  41.4 us
    unnamed x133, local copies, waits for them, and re-layouts  34.3 us
    ppermute x12, waiting for transfers between devices, passed_along(): return lax.ppermute(block, axis, route)  21.7 us
    slice x3, local copies, waits for them, and re-layouts, with_rims(): taller[:, :, :, 0].reshape(-1)  7.28 us
    slice x3, local copies, waits for them, and re-layouts, with_rims(): taller[:, :, :, slab_cols - 1].reshape(-1)  7.27 us
    dot_general x2, matrix products, window_conv(): jnp.einsum('eqim,exmpl->qxipl', filter_weight, window_patches, preferred_...  5.04 us
    concatenate x2, local copies, waits for them, and re-layouts, window_conv(): jnp.concatenate([column_span[2][..., 1:], right_term[..., None]], axis=-1)  4.38 us
  transfers between devices with their start and end apart: 12, of which 6 were waited for; matrix products, arithmetic and copies ran while one was open for 33% of the time, Pallas kernels for 0%

commit v1 on v0

v1 whole, which is shorter than its diff:
```python
import functools

import jax
import jax.numpy as jnp
from jax import lax
from jax.experimental import pallas as pl
from jax.experimental.pallas import tpu as pltpu
from jax.sharding import PartitionSpec as P

GRID_COLUMN_COUNT = 8
MESH = pl.DeviceIdType.MESH
norm_eps = 1e-06
f32 = jnp.float32
bf16 = jnp.bfloat16

COPIES = 32


def kernel(
    grid_cols,
    grid_rows,
    groups,
    links,
    extents,
    x_hbm,
    g1_hbm,
    w1_hbm,
    b1_hbm,
    g2_hbm,
    w2_hbm,
    b2_hbm,
    wd_hbm,
    bd_hbm,
    out_hbm,
    x_raw,
    spread,
    x_rows,
    w_raw,
    wd_raw,
    vec_raw,
    vecs,
    w_conv,
    w_down,
    act1,
    act2,
    block,
    sums,
    edge_part,
    edge_sum,
    edge_out,
    edge_left,
    edge_right,
    result,
    load_sem,
    send_sem,
    recv_sem,
    store_sem,
):
    channels = vecs.shape[1]
    tile = lax.axis_index("tile")
    group = lax.axis_index("tm")
    grow, gcol = tile // grid_cols, tile % grid_cols
    up = (((grow + grid_rows - 1) % grid_rows) * grid_cols + gcol, group)
    down = (((grow + 1) % grid_rows) * grid_cols + gcol, group)
    left = (grow * grid_cols + (gcol + grid_cols - 1) % grid_cols, group)
    right = (grow * grid_cols + (gcol + 1) % grid_cols, group)
    later = (tile, (group + 1) % groups)
    before = (tile, (group + groups - 1) % groups)

    barrier = pltpu.get_barrier_semaphore()
    for device in (up, down, left, right, later, before):
        pl.semaphore_signal(barrier, inc=1, device_id=device, device_id_type=MESH)

    loads = []

    def load(src, dst):
        copy = pltpu.make_async_copy(src, dst, load_sem.at[len(loads)])
        copy.start()
        loads.append(copy)
        return copy

    x_loads = {t: load(x_hbm.at[t], x_raw.at[t]) for t in (2, 3, 0, 1)}
    vec_loads = [
        load(ref, vec_raw.at[i]) for i, ref in enumerate((g1_hbm, b1_hbm, g2_hbm, b2_hbm, bd_hbm))
    ]
    w1_load = load(w1_hbm, w_raw.at[0])
    w2_load = load(w2_hbm, w_raw.at[1])
    wd_load = load(wd_hbm, wd_raw)

    sends = []

    def send(src, dst, device):
        i = len(sends)
        copy = pltpu.make_async_remote_copy(
            src_ref=src,
            dst_ref=dst,
            send_sem=send_sem.at[i],
            recv_sem=recv_sem.at[i],
            device_id=device,
            device_id_type=MESH,
        )
        copy.start()
        sends.append(copy)
        return copy

    lane = lax.broadcasted_iota(jnp.int32, (channels, 128), 1)
    lane_row = lax.broadcasted_iota(jnp.int32, (1, 128), 1)
    up_ok, down_ok = links[0, 0] >= 0, links[0, 1] >= 0
    left_ok, right_ok = links[0, 2] >= 0, links[0, 3] >= 0
    row_count, col_count = extents[0, 0], extents[0, 1]

    def inside(r):
        cols = jnp.where(r < row_count, col_count, 0)
        return (lane_row < cols).astype(f32)

    def activate(values, gain, r):
        mean_square = jnp.mean(values * values, axis=0, keepdims=True)
        normed = values * lax.rsqrt(mean_square + norm_eps) * gain
        return (normed / (1.0 + jnp.exp(-normed)) * inside(r)).astype(bf16)

    for copy in vec_loads:
        copy.wait()
    diagonal = lax.broadcasted_iota(jnp.int32, (channels, channels), 0) == lax.broadcasted_iota(
        jnp.int32, (channels, channels), 1
    )
    for i in range(5):
        column = jnp.sum(jnp.where(diagonal, vec_raw[i], 0.0), axis=1, keepdims=True)
        vecs[i] = jnp.broadcast_to(column, (channels, 128))

    def first(t):
        x_loads[t].wait()
        spread[...] = x_raw[t].astype(f32)
        gain = vecs[0]
        for r in range(4):
            values = spread[pl.ds(r, channels, stride=4), :]
            x_rows[t, r] = values.astype(bf16)
            act1[2 + t, 1 + r] = activate(values, gain, r)

    def masked(ref, index, ok):
        ref[index] = jnp.where(ok, ref[index], jnp.zeros_like(ref[index]))

    def send_frames(act):
        return [
            send(act.at[4, pl.ds(1, 4)], act.at[0, pl.ds(1, 4)], later),
            send(act.at[5, pl.ds(1, 4)], act.at[1, pl.ds(1, 4)], later),
        ]

    def send_rows(act, f):
        frames = pl.ds(f, 2)
        return [
            send(act.at[frames, 4], act.at[frames, 0], down),
            send(act.at[frames, 1], act.at[frames, 5], up),
        ]

    def wait_rows(act, f, copies):
        copies[0].wait_recv()
        copies[1].wait_recv()
        for g in (f, f + 1):
            masked(act, (g, 0), up_ok)
            masked(act, (g, 5), down_ok)

    def edges(act, frames, rows, total):
        for f in frames:
            for r in rows:
                k = f * 6 + r
                moved = pltpu.roll(act[f, r].astype(f32), 2 * k + 1, 1)
                total = jnp.where(lane // 2 == k, moved, total)
        return total

    def send_edges(slot, total):
        edge_out[slot] = total.astype(bf16)
        return [
            send(edge_out.at[slot], edge_left.at[slot], right),
            send(edge_out.at[slot], edge_right.at[slot], left),
        ]

    def patches(act, t, r):
        return jnp.concatenate(
            [act[t + dt, r : r + 3].reshape(3 * channels, 128) for dt in range(3)], axis=0
        )

    def products(act, weight, t, rows):
        operand = jnp.concatenate([patches(act, t, r) for r in rows], axis=1)
        total = jnp.dot(weight[...], operand, preferred_element_type=f32)
        for i, r in enumerate(rows):
            sums[t, r] = total[:, 128 * i : 128 * i + 128]

    def received(slot):
        both = jnp.where(
            lane % 2 == 0,
            jnp.where(left_ok, edge_left[slot].astype(f32), 0.0),
            jnp.where(right_ok, edge_right[slot].astype(f32), 0.0),
        )
        return both

    def edge_products(cells, weight):
        operand = jnp.concatenate(
            [
                cells if dt + dr == 0 else pltpu.roll(cells, 128 - 2 * (6 * dt + dr), 1)
                for dt in range(3)
                for dr in range(3)
            ],
            axis=0,
        ).astype(bf16)
        west = jnp.dot(weight[:channels], operand, preferred_element_type=f32)
        east = jnp.dot(weight[2 * channels :], operand, preferred_element_type=f32)
        edge_sum[...] = jnp.where(
            lane % 2 == 1, pltpu.roll(west, 1, 1), pltpu.roll(east, 127, 1)
        )

    def convolved(t, r):
        k = 6 * t + r
        ends = pltpu.roll(edge_sum[...], 128 - (2 * k + 1), 1)
        west = jnp.where(lane == 0, ends, pltpu.roll(sums[t, r, :channels], 1, 1))
        east = jnp.where(lane == 127, ends, pltpu.roll(sums[t, r, 2 * channels :], 127, 1))
        return west + sums[t, r, channels : 2 * channels] + east

    def arrange(raw, taps, step, store):
        value = raw.astype(f32)
        for dc in range(3):
            parts = [
                value[:, (3 * tap + dc) * channels : (3 * tap + dc + 1) * channels]
                for tap in range(taps)
            ]
            store(dc, jnp.concatenate(parts, axis=1).astype(bf16))

    def store_conv(i):
        def put(dc, rows):
            w_conv[i, dc * channels : (dc + 1) * channels] = rows

        return put

    def store_down(dc, rows):
        w_down[dc * channels : (dc + 1) * channels] = rows

    zeros = jnp.zeros((channels, 128), f32)

    def conv_layer(layer, act, frame_copies, row_copies, finish_late, finish_early):
        weight = w_conv.at[layer]
        products(act, weight, 2, (1, 2))
        products(act, weight, 3, (1, 2))
        edge_part[...] = edges(act, range(2, 6), range(1, 5), zeros)
        for f in (4, 2):
            wait_rows(act, f, row_copies[f])
        own_edges = send_edges(2 * layer, edges(act, range(2, 6), (0, 5), edge_part[...]))
        products(act, weight, 2, (0, 3))
        products(act, weight, 3, (0, 3))
        own_edges[0].wait_recv()
        own_edges[1].wait_recv()
        own_cells = received(2 * layer)
        edge_part[...] = own_cells
        edge_products(own_cells, weight)
        finish_late()
        for i, copy in enumerate(frame_copies):
            copy.wait_recv()
            masked(act, (i, slice(1, 5)), group > 0)
        history_rows = send_rows(act, 0)
        history_part = edges(act, range(2), range(1, 5), zeros)
        products(act, weight, 0, (1, 2))
        products(act, weight, 1, (1, 2))
        wait_rows(act, 0, history_rows)
        history_edges = send_edges(2 * layer + 1, edges(act, range(2), (0, 5), history_part))
        products(act, weight, 0, (0, 3))
        products(act, weight, 1, (0, 3))
        history_edges[0].wait_recv()
        history_edges[1].wait_recv()
        edge_products(
            jnp.where(lane < 24, received(2 * layer + 1), edge_part[...]), weight
        )
        finish_early()

    first(2)
    first(3)
    pl.semaphore_wait(barrier, 6)
    frames1 = send_frames(act1)
    rows1 = {4: send_rows(act1, 4)}
    first(0)
    first(1)
    rows1[2] = send_rows(act1, 2)
    w1_load.wait()
    arrange(w_raw[0], 9, 3, store_conv(0))

    rows2 = {}
    frames2 = []

    def second(t):
        for r in range(4):
            act2[2 + t, 1 + r] = activate(convolved(t, r) + vecs[1], vecs[2], r)

    def second_late():
        second(2)
        second(3)
        frames2.extend(send_frames(act2))
        rows2[4] = send_rows(act2, 4)

    def second_early():
        second(0)
        second(1)
        rows2[2] = send_rows(act2, 2)
        w2_load.wait()
        arrange(w_raw[1], 9, 3, store_conv(1))

    conv_layer(0, act1, frames1, rows1, second_late, second_early)

    block_rows = []

    def third(t):
        for r in range(4):
            total = x_rows[t, r].astype(f32) + (convolved(t, r) + vecs[3])
            block[t, r] = (total * inside(r)).astype(bf16)

    def send_block(t):
        frames = pl.ds(t, 2)
        block_rows.append((t, send(block.at[frames, 0], block.at[frames, 4], up)))

    def third_late():
        third(2)
        third(3)
        send_block(2)
        wd_load.wait()
        arrange(wd_raw[...], 3, 1, store_down)

    def third_early():
        third(0)
        third(1)
        send_block(0)

    conv_layer(1, act2, frames2, rows2, third_late, third_early)

    def block_edges(rows, total):
        for t in range(4):
            for r in rows:
                k = t * 5 + r
                value = block[t, r].astype(f32)
                total = jnp.where(lane == k, value if k == 0 else pltpu.roll(value, k, 1), total)
        return total

    edge_cells = block_edges(range(4), zeros)
    for t, copy in block_rows:
        copy.wait_recv()
        for u in (t, t + 1):
            masked(block, (u, 4), down_ok)
    edge_out[4] = block_edges((4,), edge_cells).astype(bf16)
    corner = send(edge_out.at[4], edge_right.at[4], left)
    for t in range(4):
        operand = jnp.concatenate(
            [block[t, 2 * i : 2 * i + 3].reshape(3 * channels, 128) for i in range(2)], axis=1
        )
        total = jnp.dot(w_down[...], operand, preferred_element_type=f32)
        for i in range(2):
            sums[t, i] = total[:, 128 * i : 128 * i + 128]
    corner.wait_recv()
    cells = jnp.where(right_ok, edge_right[4].astype(f32), 0.0)
    operand = jnp.concatenate(
        [cells] + [pltpu.roll(cells, 128 - dr, 1) for dr in (1, 2)], axis=0
    ).astype(bf16)
    east = jnp.dot(w_down[2 * channels :], operand, preferred_element_type=f32)
    picked = (
        lax.broadcasted_iota(jnp.int32, (256, 128), 0)
        == 2 * lax.broadcasted_iota(jnp.int32, (256, 128), 1)
    ).astype(f32).astype(bf16)
    col_limit = jnp.where(right_ok, 1024, col_count)
    stores = []
    for t in range(4):
        halves = []
        for i in range(2):
            row_limit = jnp.where(down_ok, 1024, row_count)
            limit = jnp.where(2 * i + 2 <= row_limit, col_limit, 0)
            keep = (lane_row + 2 <= limit).astype(f32)
            ends = pltpu.roll(east, 126 - (5 * t + 2 * i), 1)
            total = (
                sums[t, i, :channels]
                + pltpu.roll(sums[t, i, channels : 2 * channels], 127, 1)
                + jnp.where(lane == 126, ends, pltpu.roll(sums[t, i, 2 * channels :], 126, 1))
            )
            halves.append(((total + vecs[4]) * keep).astype(bf16))
        result[t] = jnp.dot(
            jnp.concatenate(halves, axis=1), picked, preferred_element_type=f32
        ).astype(bf16)
        copy = pltpu.make_async_copy(result.at[t], out_hbm.at[t], store_sem.at[t])
        copy.start()
        stores.append(copy)
    for copy in sends:
        copy.wait_send()
    for copy in stores:
        copy.wait()


def per_device(grid_rows, groups, video, links, extents, g1, w1, b1, g2, w2, b2, wd, bd):
    _, frames, channels, slab_rows, slab_cols = video.shape
    x = video.reshape(frames, channels * slab_rows, slab_cols)
    vectors = [v.reshape(1, channels) for v in (g1, b1, g2, b2, bd)]
    g1, b1, g2, b2, bd = vectors
    vmem = pltpu.VMEM
    field = (6, 6, channels, 128)
    out = pl.pallas_call(
        functools.partial(kernel, GRID_COLUMN_COUNT, grid_rows, groups),
        out_shape=jax.ShapeDtypeStruct((frames, channels, 128), bf16),
        in_specs=[pl.BlockSpec(memory_space=pltpu.SMEM)] * 2
        + [pl.BlockSpec(memory_space=pl.ANY)] * 9,
        out_specs=pl.BlockSpec(memory_space=pl.ANY),
        scratch_shapes=[
            vmem((4, channels * 4, 128), bf16),
            vmem((channels * 4, 128), f32),
            vmem((4, 4, channels, 128), bf16),
            vmem((2, channels, 27 * channels), bf16),
            vmem((channels, 9 * channels), bf16),
            vmem((5, 1, channels), f32),
            vmem((5, channels, 128), f32),
            vmem((2, 3 * channels, 9 * channels), bf16),
            vmem((3 * channels, 3 * channels), bf16),
            vmem(field, bf16),
            vmem(field, bf16),
            vmem((4, 5, channels, 128), bf16),
            vmem((4, 4, 3 * channels, 128), f32),
            vmem((channels, 128), f32),
            vmem((channels, 128), f32),
            vmem((5, channels, 128), bf16),
            vmem((4, channels, 128), bf16),
            vmem((5, channels, 128), bf16),
            vmem((4, channels, 128), bf16),
            pltpu.SemaphoreType.DMA((12,)),
            pltpu.SemaphoreType.DMA((COPIES,)),
            pltpu.SemaphoreType.DMA((COPIES,)),
            pltpu.SemaphoreType.DMA((4,)),
        ],
        compiler_params=pltpu.CompilerParams(
            collective_id=0, has_side_effects=True, vmem_limit_bytes=60 * 2**20
        ),
    )(links, extents, x, g1, w1, b1, g2, w2, b2, wd, bd)
    return out[None]


def solution(mesh):
    placed = (P("tile", "tm", None, None, None), P("tile", None), P("tile", None)) + (P(),) * 8
    return jax.shard_map(
        functools.partial(
            per_device, mesh.shape["tile"] // GRID_COLUMN_COUNT, mesh.shape["tm"]
        ),
        mesh=mesh,
        in_specs=placed,
        out_specs=P("tile", "tm", None, None),
        check_vma=False,
    )
```

time: 176 us -> 51.2 us (0.29)
  the two profiles are of different devices: /device:TPU:223 before, /device:TPU:1 now
where the time goes in v1:
time: 51.2 us; the launch traced here: 51 us
  Pallas kernels  49.5 us (97%)
  local copies, waits for them, and re-layouts  1.54 us (3%)
    pallas_call x1, Pallas kernels, per_device(): pl.pallas_call(functools.partial(kernel, GRID_COLUMN_COUNT, grid_rows, gr...  49.5 us
    unnamed x1, local copies, waits for them, and re-layouts  1.54 us

profile of v1, /device:TPU:1, one launch (start us, length us, event | category | flops | bytes accessed | tf_op | source)
XLA Modules:
  0.0 51.0 jit_solution(5642213144309835216)
XLA Ops:
  0.0 49.5 %shard_map.109 = bf16[4,96,128]{2,1,0:T(8,128)(2,1)} custom-call(s32[1,4]{1,0:T(1,128)} %links.1, s32[1,2]{1,0:T(1,128)} %extents.1, bf16[4,384,128]{2,1,0:T(8,128)(2,1)} %bitcast.7, f32[1,96]{1,0:T(1,128)} %bitcast.9, bf16[96,2592]{1,0:T(8,128)(2,1)} %w1_hbm.1, f32[1,96]{1,0:T(1,128)} %bitcast.10, f32[1,96]{1,0:T(1,128)} %bitcast.11, ...), custom_call_target="tpu_custom_call" | custom-call | tf_op jit(solution)/shard_map/pallas_call | solution.py:396
  49.5 1.5 %copy.13 = bf16[1,4,96,128]{3,2,1,0:T(8,128)(2,1)} copy(bf16[1,4,96,128]{3,2,1,0:T(8,128)(2,1)} %bitcast.8) | data formatting | bytes 196608

commit v2 on v1

--- a/solution.py
+++ b/solution.py
@@ -13,7 +13,7 @@
 f32 = jnp.float32
 bf16 = jnp.bfloat16
 
-COPIES = 32
+COPIES = 48
 
 
 def kernel(
@@ -45,11 +45,13 @@
     act2,
     block,
     sums,
-    edge_part,
     edge_sum,
+    edge_own,
     edge_out,
-    edge_left,
-    edge_right,
+    edge_side,
+    edge_corner,
+    edge_on,
+    edge_past,
     result,
     load_sem,
     send_sem,
@@ -60,15 +62,18 @@
     tile = lax.axis_index("tile")
     group = lax.axis_index("tm")
     grow, gcol = tile // grid_cols, tile % grid_cols
-    up = (((grow + grid_rows - 1) % grid_rows) * grid_cols + gcol, group)
-    down = (((grow + 1) % grid_rows) * grid_cols + gcol, group)
-    left = (grow * grid_cols + (gcol + grid_cols - 1) % grid_cols, group)
-    right = (grow * grid_cols + (gcol + 1) % grid_cols, group)
+    def slab(rows, cols):
+        row = (grow + rows + grid_rows) % grid_rows
+        return (row * grid_cols + (gcol + cols + grid_cols) % grid_cols, group)
+
+    up, down, left, right = slab(-1, 0), slab(1, 0), slab(0, -1), slab(0, 1)
+    up_left, up_right, down_left, down_right = slab(-1, -1), slab(-1, 1), slab(1, -1), slab(1, 1)
     later = (tile, (group + 1) % groups)
     before = (tile, (group + groups - 1) % groups)
+    around = (up, down, left, right, up_left, up_right, down_left, down_right, later, before)
 
     barrier = pltpu.get_barrier_semaphore()
-    for device in (up, down, left, right, later, before):
+    for device in around:
         pl.semaphore_signal(barrier, inc=1, device_id=device, device_id_type=MESH)
 
     loads = []
@@ -139,12 +144,6 @@
     def masked(ref, index, ok):
         ref[index] = jnp.where(ok, ref[index], jnp.zeros_like(ref[index]))
 
-    def send_frames(act):
-        return [
-            send(act.at[4, pl.ds(1, 4)], act.at[0, pl.ds(1, 4)], later),
-            send(act.at[5, pl.ds(1, 4)], act.at[1, pl.ds(1, 4)], later),
-        ]
-
     def send_rows(act, f):
         frames = pl.ds(f, 2)
         return [
@@ -153,26 +152,76 @@
         ]
 
     def wait_rows(act, f, copies):
-        copies[0].wait_recv()
-        copies[1].wait_recv()
+        for copy in copies:
+            copy.wait_recv()
         for g in (f, f + 1):
             masked(act, (g, 0), up_ok)
             masked(act, (g, 5), down_ok)
 
-    def edges(act, frames, rows, total):
-        for f in frames:
-            for r in rows:
-                k = f * 6 + r
-                moved = pltpu.roll(act[f, r].astype(f32), 2 * k + 1, 1)
+    def send_past_rims(act):
+        return [
+            send(act.at[pl.ds(4, 2), 0], act.at[pl.ds(0, 2), 0], later),
+            send(act.at[pl.ds(4, 2), 5], act.at[pl.ds(0, 2), 5], later),
+        ]
+
+    def turned(total):
+        pad = jnp.zeros((128 - channels, 128), f32)
+        return jnp.concatenate([total, pad], axis=0).T
+
+    def send_edges(act, slot, frames):
+        total = jnp.zeros((channels, 128), f32)
+        for t in frames:
+            for r in range(4):
+                k = r * 4 + t
+                moved = pltpu.roll(act[2 + t, 1 + r].astype(f32), 2 * k + 1, 1)
                 total = jnp.where(lane // 2 == k, moved, total)
-        return total
-
-    def send_edges(slot, total):
-        edge_out[slot] = total.astype(bf16)
+        edge_out[slot] = turned(total)[:32].astype(bf16)
+        whole, upper, lower = (
+            edge_out.at[slot],
+            edge_out.at[slot, pl.ds(0, 16)],
+            edge_out.at[slot, pl.ds(16, 16)],
+        )
         return [
-            send(edge_out.at[slot], edge_left.at[slot], right),
-            send(edge_out.at[slot], edge_right.at[slot], left),
+            send(whole, edge_side.at[0, slot], right),
+            send(whole, edge_side.at[1, slot], left),
+            send(lower, edge_corner.at[0, slot], down_right),
+            send(lower, edge_corner.at[1, slot], down_left),
+            send(upper, edge_corner.at[2, slot], up_right),
+            send(upper, edge_corner.at[3, slot], up_left),
         ]
+
+    def chosen(even, even_ok, odd, odd_ok):
+        odd_row = lax.broadcasted_iota(jnp.int32, even.shape, 0) % 2 == 1
+        even = jnp.where(even_ok, even.astype(f32), 0.0)
+        return jnp.where(odd_row, jnp.where(odd_ok, odd.astype(f32), 0.0), even)
+
+    def sides(slot):
+        return chosen(edge_side[0, slot], left_ok, edge_side[1, slot], right_ok)
+
+    def upper_corners(slot):
+        return chosen(
+            edge_corner[0, slot], up_ok & left_ok, edge_corner[1, slot], up_ok & right_ok
+        )[8:]
+
+    def lower_corners(slot):
+        return chosen(
+            edge_corner[2, slot], down_ok & left_ok, edge_corner[3, slot], down_ok & right_ok
+        )[:8]
+
+    def whole_edges(slot):
+        return jnp.concatenate([upper_corners(slot), sides(slot), lower_corners(slot)], axis=0)
+
+    def edge_cells(own, past):
+        first_half = lax.broadcasted_iota(jnp.int32, (8, 128), 0) < 4
+        pieces = []
+        for row in range(6):
+            mine = pltpu.roll(own[8 * row : 8 * row + 8], 4, 0)
+            theirs = 0.0
+            if past is not None:
+                theirs = pltpu.roll(past[8 * row : 8 * row + 8], 4, 0)
+            pieces += [jnp.where(first_half, theirs, mine), jnp.where(first_half, mine, 0.0)]
+        pieces.append(jnp.zeros((32, 128), f32))
+        return jnp.concatenate(pieces, axis=0).T[:channels]
 
     def patches(act, t, r):
         return jnp.concatenate(
@@ -185,18 +234,10 @@
         for i, r in enumerate(rows):
             sums[t, r] = total[:, 128 * i : 128 * i + 128]
 
-    def received(slot):
-        both = jnp.where(
-            lane % 2 == 0,
-            jnp.where(left_ok, edge_left[slot].astype(f32), 0.0),
-            jnp.where(right_ok, edge_right[slot].astype(f32), 0.0),
-        )
-        return both
-
     def edge_products(cells, weight):
         operand = jnp.concatenate(
             [
-                cells if dt + dr == 0 else pltpu.roll(cells, 128 - 2 * (6 * dt + dr), 1)
+                cells if dt + dr == 0 else pltpu.roll(cells, 128 - (16 * dr + 2 * dt), 1)
                 for dt in range(3)
                 for dr in range(3)
             ],
@@ -209,8 +250,8 @@
         )
 
     def convolved(t, r):
-        k = 6 * t + r
-        ends = pltpu.roll(edge_sum[...], 128 - (2 * k + 1), 1)
+        k = 16 * r + 2 * t
+        ends = pltpu.roll(edge_sum[...], 128 - (k + 1), 1)
         west = jnp.where(lane == 0, ends, pltpu.roll(sums[t, r, :channels], 1, 1))
         east = jnp.where(lane == 127, ends, pltpu.roll(sums[t, r, 2 * channels :], 127, 1))
         return west + sums[t, r, channels : 2 * channels] + east
@@ -233,115 +274,127 @@
     def store_down(dc, rows):
         w_down[dc * channels : (dc + 1) * channels] = rows
 
-    zeros = jnp.zeros((channels, 128), f32)
-
-    def conv_layer(layer, act, frame_copies, row_copies, finish_late, finish_early):
-        weight = w_conv.at[layer]
-        products(act, weight, 2, (1, 2))
-        products(act, weight, 3, (1, 2))
-        edge_part[...] = edges(act, range(2, 6), range(1, 5), zeros)
-        for f in (4, 2):
-            wait_rows(act, f, row_copies[f])
-        own_edges = send_edges(2 * layer, edges(act, range(2, 6), (0, 5), edge_part[...]))
-        products(act, weight, 2, (0, 3))
-        products(act, weight, 3, (0, 3))
-        own_edges[0].wait_recv()
-        own_edges[1].wait_recv()
-        own_cells = received(2 * layer)
-        edge_part[...] = own_cells
-        edge_products(own_cells, weight)
-        finish_late()
-        for i, copy in enumerate(frame_copies):
-            copy.wait_recv()
-            masked(act, (i, slice(1, 5)), group > 0)
-        history_rows = send_rows(act, 0)
-        history_part = edges(act, range(2), range(1, 5), zeros)
-        products(act, weight, 0, (1, 2))
-        products(act, weight, 1, (1, 2))
-        wait_rows(act, 0, history_rows)
-        history_edges = send_edges(2 * layer + 1, edges(act, range(2), (0, 5), history_part))
-        products(act, weight, 0, (0, 3))
-        products(act, weight, 1, (0, 3))
-        history_edges[0].wait_recv()
-        history_edges[1].wait_recv()
-        edge_products(
-            jnp.where(lane < 24, received(2 * layer + 1), edge_part[...]), weight
-        )
-        finish_early()
-
-    first(2)
-    first(3)
-    pl.semaphore_wait(barrier, 6)
-    frames1 = send_frames(act1)
-    rows1 = {4: send_rows(act1, 4)}
-    first(0)
-    first(1)
-    rows1[2] = send_rows(act1, 2)
-    w1_load.wait()
-    arrange(w_raw[0], 9, 3, store_conv(0))
-
-    rows2 = {}
-    frames2 = []
-
-    def second(t):
-        for r in range(4):
+    def second(t, rows):
+        for r in rows:
             act2[2 + t, 1 + r] = activate(convolved(t, r) + vecs[1], vecs[2], r)
-
-    def second_late():
-        second(2)
-        second(3)
-        frames2.extend(send_frames(act2))
-        rows2[4] = send_rows(act2, 4)
-
-    def second_early():
-        second(0)
-        second(1)
-        rows2[2] = send_rows(act2, 2)
-        w2_load.wait()
-        arrange(w_raw[1], 9, 3, store_conv(1))
-
-    conv_layer(0, act1, frames1, rows1, second_late, second_early)
-
-    block_rows = []
 
     def third(t):
         for r in range(4):
             total = x_rows[t, r].astype(f32) + (convolved(t, r) + vecs[3])
             block[t, r] = (total * inside(r)).astype(bf16)
 
-    def send_block(t):
-        frames = pl.ds(t, 2)
-        block_rows.append((t, send(block.at[frames, 0], block.at[frames, 4], up)))
-
-    def third_late():
-        third(2)
-        third(3)
-        send_block(2)
-        wd_load.wait()
-        arrange(wd_raw[...], 3, 1, store_down)
-
-    def third_early():
-        third(0)
-        third(1)
-        send_block(0)
-
-    conv_layer(1, act2, frames2, rows2, third_late, third_early)
-
-    def block_edges(rows, total):
-        for t in range(4):
-            for r in rows:
-                k = t * 5 + r
-                value = block[t, r].astype(f32)
-                total = jnp.where(lane == k, value if k == 0 else pltpu.roll(value, k, 1), total)
-        return total
-
-    edge_cells = block_edges(range(4), zeros)
-    for t, copy in block_rows:
+    late, early, middle, outer = (2, 3), (0, 1), (1, 2), (0, 3)
+    past_frames = pl.ds(0, 2)
+    new_frames = pl.ds(4, 2)
+
+    for t in (2, 3, 0, 1):
+        first(t)
+    w1_load.wait()
+    arrange(w_raw[0], 9, 3, store_conv(0))
+    pl.semaphore_wait(barrier, len(around))
+
+    edges1 = send_edges(act1, 0, range(4))
+    rows1 = send_rows(act1, 4) + send_rows(act1, 2)
+    past1 = [
+        send(act1.at[4, pl.ds(1, 4)], act1.at[0, pl.ds(1, 4)], later),
+        send(act1.at[5, pl.ds(1, 4)], act1.at[1, pl.ds(1, 4)], later),
+    ]
+    weight1, weight2 = w_conv.at[0], w_conv.at[1]
+
+    for t in late:
+        products(act1, weight1, t, middle)
+    for copy in edges1[:2]:
         copy.wait_recv()
-        for u in (t, t + 1):
-            masked(block, (u, 4), down_ok)
-    edge_out[4] = block_edges((4,), edge_cells).astype(bf16)
-    corner = send(edge_out.at[4], edge_right.at[4], left)
+    no_rows = jnp.zeros((8, 128), f32)
+    edge_products(
+        edge_cells(jnp.concatenate([no_rows, sides(0), no_rows], axis=0), None), weight1
+    )
+    for t in late:
+        second(t, middle)
+    past2 = [send(act2.at[new_frames, pl.ds(2, 2)], act2.at[past_frames, pl.ds(2, 2)], later)]
+    wait_rows(act1, 4, rows1[:2])
+    past1 += send_past_rims(act1)
+    wait_rows(act1, 2, rows1[2:])
+    for copy in edges1[2:]:
+        copy.wait_recv()
+    own = whole_edges(0)
+    edge_own[...] = own
+    edge_on[0] = own.astype(bf16)
+    past1.append(send(edge_on.at[0], edge_past.at[0], later))
+    for t in late:
+        products(act1, weight1, t, outer)
+    edge_products(edge_cells(own, None), weight1)
+    for t in late:
+        second(t, outer)
+    past2 += [
+        send(act2.at[new_frames, 1], act2.at[past_frames, 1], later),
+        send(act2.at[new_frames, 4], act2.at[past_frames, 4], later),
+    ]
+    rows2 = send_rows(act2, 4)
+    edges2 = send_edges(act2, 1, late)
+    w2_load.wait()
+    arrange(w_raw[1], 9, 3, store_conv(1))
+    wd_load.wait()
+    arrange(wd_raw[...], 3, 1, store_down)
+    wait_rows(act2, 4, rows2)
+    past2 += send_past_rims(act2)
+    for copy in edges2:
+        copy.wait_recv()
+    late_edges = whole_edges(1)
+    edge_on[1] = late_edges.astype(bf16)
+    past2.append(send(edge_on.at[1], edge_past.at[1], later))
+
+    def take_past(act, copies):
+        for copy in copies:
+            copy.wait_recv()
+        for f in (0, 1):
+            masked(act, f, group > 0)
+
+    def past_edges(layer):
+        return jnp.where(group > 0, edge_past[layer].astype(f32), 0.0)
+
+    take_past(act1, past1)
+    for t in early:
+        products(act1, weight1, t, middle)
+        products(act1, weight1, t, outer)
+    edge_products(edge_cells(edge_own[...], past_edges(0)), weight1)
+    edge_own[...] = late_edges
+    for t in early:
+        second(t, range(4))
+    rows2 = send_rows(act2, 2)
+    edges2 = send_edges(act2, 2, early)
+
+    for t in late:
+        products(act2, weight2, t, middle)
+    wait_rows(act2, 2, rows2)
+    for t in late:
+        products(act2, weight2, t, outer)
+    for copy in edges2:
+        copy.wait_recv()
+    late_row = lax.broadcasted_iota(jnp.int32, (48, 128), 0) % 8 >= 4
+    edge_own[...] = jnp.where(late_row, edge_own[...], whole_edges(2))
+    take_past(act2, past2)
+    for t in early:
+        products(act2, weight2, t, middle)
+        products(act2, weight2, t, outer)
+    edge_products(edge_cells(edge_own[...], past_edges(1)), weight2)
+    for t in range(4):
+        third(t)
+    low_rows = send(block.at[:, 0], block.at[:, 4], up)
+    total = jnp.zeros((channels, 128), f32)
+    for t in range(4):
+        for r in range(4):
+            k = r * 4 + t
+            value = block[t, r].astype(f32)
+            total = jnp.where(lane == k, value if k == 0 else pltpu.roll(value, k, 1), total)
+    edge_out[3] = turned(total)[:32].astype(bf16)
+    corners = [
+        send(edge_out.at[3, pl.ds(0, 16)], edge_side.at[1, 3, pl.ds(0, 16)], left),
+        send(edge_out.at[3, pl.ds(0, 16)], edge_corner.at[3, 3], up_left),
+    ]
+    low_rows.wait_recv()
+    for t in range(4):
+        masked(block, (t, 4), down_ok)
     for t in range(4):
         operand = jnp.concatenate(
             [block[t, 2 * i : 2 * i + 3].reshape(3 * channels, 128) for i in range(2)], axis=1
@@ -349,10 +402,18 @@
         total = jnp.dot(w_down[...], operand, preferred_element_type=f32)
         for i in range(2):
             sums[t, i] = total[:, 128 * i : 128 * i + 128]
-    corner.wait_recv()
-    cells = jnp.where(right_ok, edge_right[4].astype(f32), 0.0)
+    for copy in corners:
+        copy.wait_recv()
+    cells = jnp.concatenate(
+        [
+            jnp.where(right_ok, edge_side[1, 3].astype(f32)[:16], 0.0),
+            jnp.where(right_ok & down_ok, edge_corner[3, 3].astype(f32)[:8], 0.0),
+            jnp.zeros((104, 128), f32),
+        ],
+        axis=0,
+    ).T[:channels]
     operand = jnp.concatenate(
-        [cells] + [pltpu.roll(cells, 128 - dr, 1) for dr in (1, 2)], axis=0
+        [cells] + [pltpu.roll(cells, 128 - 4 * dr, 1) for dr in (1, 2)], axis=0
     ).astype(bf16)
     east = jnp.dot(w_down[2 * channels :], operand, preferred_element_type=f32)
     picked = (
@@ -367,7 +428,7 @@
             row_limit = jnp.where(down_ok, 1024, row_count)
             limit = jnp.where(2 * i + 2 <= row_limit, col_limit, 0)
             keep = (lane_row + 2 <= limit).astype(f32)
-            ends = pltpu.roll(east, 126 - (5 * t + 2 * i), 1)
+            ends = pltpu.roll(east, 126 - (8 * i + t), 1)
             total = (
                 sums[t, i, :channels]
                 + pltpu.roll(sums[t, i, channels : 2 * channels], 127, 1)
@@ -414,10 +475,12 @@
             vmem((4, 5, channels, 128), bf16),
             vmem((4, 4, 3 * channels, 128), f32),
             vmem((channels, 128), f32),
-            vmem((channels, 128), f32),
-            vmem((5, channels, 128), bf16),
-            vmem((4, channels, 128), bf16),
-            vmem((5, channels, 128), bf16),
+            vmem((48, 128), f32),
+            vmem((4, 32, 128), bf16),
+            vmem((2, 4, 32, 128), bf16),
+            vmem((4, 4, 16, 128), bf16),
+            vmem((2, 48, 128), bf16),
+            vmem((2, 48, 128), bf16),
             vmem((4, channels, 128), bf16),
             pltpu.SemaphoreType.DMA((12,)),
             pltpu.SemaphoreType.DMA((COPIES,)),

time: 51.2 us -> 40.8 us (0.80)
  Pallas kernels: 49.5 us -> 39.1 us
    pallas_call x1, Pallas kernels: 49.5 us -> 39.1 us  [per_device(): pl.pallas_call(functools.partial(kernel, GRID_COLUMN_COUNT, grid_rows, gr...]
where the time goes in v2:
time: 40.8 us; the launch traced here: 40.6 us
  Pallas kernels  39.1 us (96%)
  local copies, waits for them, and re-layouts  1.54 us (4%)
    pallas_call x1, Pallas kernels, per_device(): pl.pallas_call(functools.partial(kernel, GRID_COLUMN_COUNT, grid_rows, gr...  39.1 us
    unnamed x1, local copies, waits for them, and re-layouts  1.54 us

profile of v2, /device:TPU:1, one launch (start us, length us, event | category | flops | bytes accessed | tf_op | source)
XLA Modules:
  0.0 40.6 jit_solution(12885090400759202464)
XLA Ops:
  0.0 39.1 %shard_map.109 = bf16[4,96,128]{2,1,0:T(8,128)(2,1)} custom-call(s32[1,4]{1,0:T(1,128)} %links.1, s32[1,2]{1,0:T(1,128)} %extents.1, bf16[4,384,128]{2,1,0:T(8,128)(2,1)} %bitcast.7, f32[1,96]{1,0:T(1,128)} %bitcast.9, bf16[96,2592]{1,0:T(8,128)(2,1)} %w1_hbm.1, f32[1,96]{1,0:T(1,128)} %bitcast.10, f32[1,96]{1,0:T(1,128)} %bitcast.11, ...), custom_call_target="tpu_custom_call" | custom-call | tf_op jit(solution)/shard_map/pallas_call | solution.py:457
  39.1 1.5 %copy.13 = bf16[1,4,96,128]{3,2,1,0:T(8,128)(2,1)} copy(bf16[1,4,96,128]{3,2,1,0:T(8,128)(2,1)} %bitcast.8) | data formatting | bytes 196608

commit v3 on v2

--- a/solution.py
+++ b/solution.py
@@ -20,8 +20,8 @@
     grid_cols,
     grid_rows,
     groups,
-    links,
-    extents,
+    links_hbm,
+    extents_hbm,
     x_hbm,
     g1_hbm,
     w1_hbm,
@@ -32,6 +32,8 @@
     wd_hbm,
     bd_hbm,
     out_hbm,
+    links,
+    extents,
     x_raw,
     spread,
     x_rows,
@@ -62,14 +64,14 @@
     tile = lax.axis_index("tile")
     group = lax.axis_index("tm")
     grow, gcol = tile // grid_cols, tile % grid_cols
-    def slab(rows, cols):
+    def slab(rows, cols, groups_on=0):
         row = (grow + rows + grid_rows) % grid_rows
-        return (row * grid_cols + (gcol + cols + grid_cols) % grid_cols, group)
+        col = (gcol + cols + grid_cols) % grid_cols
+        return (row * grid_cols + col, (group + groups_on + groups) % groups)
 
     up, down, left, right = slab(-1, 0), slab(1, 0), slab(0, -1), slab(0, 1)
     up_left, up_right, down_left, down_right = slab(-1, -1), slab(-1, 1), slab(1, -1), slab(1, 1)
-    later = (tile, (group + 1) % groups)
-    before = (tile, (group + groups - 1) % groups)
+    later, before = slab(0, 0, 1), slab(0, 0, -1)
     around = (up, down, left, right, up_left, up_right, down_left, down_right, later, before)
 
     barrier = pltpu.get_barrier_semaphore()
@@ -88,6 +90,7 @@
     vec_loads = [
         load(ref, vec_raw.at[i]) for i, ref in enumerate((g1_hbm, b1_hbm, g2_hbm, b2_hbm, bd_hbm))
     ]
+    scalar_loads = [load(links_hbm, links), load(extents_hbm, extents)]
     w1_load = load(w1_hbm, w_raw.at[0])
     w2_load = load(w2_hbm, w_raw.at[1])
     wd_load = load(wd_hbm, wd_raw)
@@ -110,6 +113,8 @@
 
     lane = lax.broadcasted_iota(jnp.int32, (channels, 128), 1)
     lane_row = lax.broadcasted_iota(jnp.int32, (1, 128), 1)
+    for copy in scalar_loads:
+        copy.wait()
     up_ok, down_ok = links[0, 0] >= 0, links[0, 1] >= 0
     left_ok, right_ok = links[0, 2] >= 0, links[0, 3] >= 0
     row_count, col_count = extents[0, 0], extents[0, 1]
@@ -123,12 +128,12 @@
         normed = values * lax.rsqrt(mean_square + norm_eps) * gain
         return (normed / (1.0 + jnp.exp(-normed)) * inside(r)).astype(bf16)
 
-    for copy in vec_loads:
-        copy.wait()
     diagonal = lax.broadcasted_iota(jnp.int32, (channels, channels), 0) == lax.broadcasted_iota(
         jnp.int32, (channels, channels), 1
     )
-    for i in range(5):
+
+    def spread_vector(i):
+        vec_loads[i].wait()
         column = jnp.sum(jnp.where(diagonal, vec_raw[i], 0.0), axis=1, keepdims=True)
         vecs[i] = jnp.broadcast_to(column, (channels, 128))
 
@@ -158,11 +163,11 @@
             masked(act, (g, 0), up_ok)
             masked(act, (g, 5), down_ok)
 
-    def send_past_rims(act):
-        return [
-            send(act.at[pl.ds(4, 2), 0], act.at[pl.ds(0, 2), 0], later),
-            send(act.at[pl.ds(4, 2), 5], act.at[pl.ds(0, 2), 5], later),
-        ]
+    def send_past_row(act, row):
+        return send(act.at[new_frames, row], act.at[past_frames, row], later)
+
+    def send_past_middle(act):
+        return send(act.at[new_frames, pl.ds(2, 2)], act.at[past_frames, pl.ds(2, 2)], later)
 
     def turned(total):
         pad = jnp.zeros((128 - channels, 128), f32)
@@ -286,20 +291,41 @@
     late, early, middle, outer = (2, 3), (0, 1), (1, 2), (0, 3)
     past_frames = pl.ds(0, 2)
     new_frames = pl.ds(4, 2)
-
+    weight1, weight2 = w_conv.at[0], w_conv.at[1]
+
+    def take_past_outer(act, copies):
+        for copy in copies:
+            copy.wait_recv()
+        for f in (0, 1):
+            for row in (1, 4):
+                masked(act, (f, row), group > 0)
+        return send_rows(act, 0)
+
+    def take_past_middle(act, copy):
+        copy.wait_recv()
+        for f in (0, 1):
+            masked(act, (f, slice(2, 4)), group > 0)
+
+    def past_edges(layer):
+        return jnp.where(group > 0, edge_past[layer].astype(f32), 0.0)
+
+    def send_past_edges(layer, cells):
+        edge_on[layer] = cells.astype(bf16)
+        return send(edge_on.at[layer], edge_past.at[layer], later)
+
+    spread_vector(0)
     for t in (2, 3, 0, 1):
         first(t)
+    pl.semaphore_wait(barrier, len(around))
+
+    rows1 = send_rows(act1, 4) + send_rows(act1, 2)
+    outer1 = [send_past_row(act1, 1), send_past_row(act1, 4)]
+    edges1 = send_edges(act1, 0, range(4))
+    middle1 = send_past_middle(act1)
     w1_load.wait()
     arrange(w_raw[0], 9, 3, store_conv(0))
-    pl.semaphore_wait(barrier, len(around))
-
-    edges1 = send_edges(act1, 0, range(4))
-    rows1 = send_rows(act1, 4) + send_rows(act1, 2)
-    past1 = [
-        send(act1.at[4, pl.ds(1, 4)], act1.at[0, pl.ds(1, 4)], later),
-        send(act1.at[5, pl.ds(1, 4)], act1.at[1, pl.ds(1, 4)], later),
-    ]
-    weight1, weight2 = w_conv.at[0], w_conv.at[1]
+    for i in range(1, 5):
+        spread_vector(i)
 
     for t in late:
         products(act1, weight1, t, middle)
@@ -311,76 +337,72 @@
     )
     for t in late:
         second(t, middle)
-    past2 = [send(act2.at[new_frames, pl.ds(2, 2)], act2.at[past_frames, pl.ds(2, 2)], later)]
-    wait_rows(act1, 4, rows1[:2])
-    past1 += send_past_rims(act1)
-    wait_rows(act1, 2, rows1[2:])
+    middle2 = send_past_middle(act2)
+    rims1 = take_past_outer(act1, outer1)
     for copy in edges1[2:]:
         copy.wait_recv()
     own = whole_edges(0)
     edge_own[...] = own
-    edge_on[0] = own.astype(bf16)
-    past1.append(send(edge_on.at[0], edge_past.at[0], later))
+    past_edges1 = send_past_edges(0, own)
+    wait_rows(act1, 4, rows1[:2])
+    wait_rows(act1, 2, rows1[2:])
     for t in late:
         products(act1, weight1, t, outer)
     edge_products(edge_cells(own, None), weight1)
     for t in late:
         second(t, outer)
-    past2 += [
-        send(act2.at[new_frames, 1], act2.at[past_frames, 1], later),
-        send(act2.at[new_frames, 4], act2.at[past_frames, 4], later),
-    ]
-    rows2 = send_rows(act2, 4)
-    edges2 = send_edges(act2, 1, late)
+    outer2 = [send_past_row(act2, 1), send_past_row(act2, 4)]
+    rows2_late = send_rows(act2, 4)
+    edges2_late = send_edges(act2, 1, late)
+
+    take_past_middle(act1, middle1)
+    for t in early:
+        products(act1, weight1, t, middle)
     w2_load.wait()
     arrange(w_raw[1], 9, 3, store_conv(1))
+    wait_rows(act1, 0, rims1)
+    for t in early:
+        products(act1, weight1, t, outer)
+    past_edges1.wait_recv()
+    edge_products(edge_cells(edge_own[...], past_edges(0)), weight1)
+    for t in early:
+        second(t, range(4))
+    rows2_early = send_rows(act2, 2)
+    edges2_early = send_edges(act2, 2, early)
+    for copy in edges2_late:
+        copy.wait_recv()
+    late_edges = whole_edges(1)
+    past_edges2 = send_past_edges(1, late_edges)
+    edge_own[...] = late_edges
+    rims2 = take_past_outer(act2, outer2)
     wd_load.wait()
     arrange(wd_raw[...], 3, 1, store_down)
-    wait_rows(act2, 4, rows2)
-    past2 += send_past_rims(act2)
-    for copy in edges2:
-        copy.wait_recv()
-    late_edges = whole_edges(1)
-    edge_on[1] = late_edges.astype(bf16)
-    past2.append(send(edge_on.at[1], edge_past.at[1], later))
-
-    def take_past(act, copies):
-        for copy in copies:
-            copy.wait_recv()
-        for f in (0, 1):
-            masked(act, f, group > 0)
-
-    def past_edges(layer):
-        return jnp.where(group > 0, edge_past[layer].astype(f32), 0.0)
-
-    take_past(act1, past1)
+
+    for t in late:
+        products(act2, weight2, t, middle)
+    take_past_middle(act2, middle2)
     for t in early:
-        products(act1, weight1, t, middle)
-        products(act1, weight1, t, outer)
-    edge_products(edge_cells(edge_own[...], past_edges(0)), weight1)
-    edge_own[...] = late_edges
-    for t in early:
-        second(t, range(4))
-    rows2 = send_rows(act2, 2)
-    edges2 = send_edges(act2, 2, early)
-
-    for t in late:
         products(act2, weight2, t, middle)
-    wait_rows(act2, 2, rows2)
+    wait_rows(act2, 4, rows2_late)
+    wait_rows(act2, 2, rows2_early)
     for t in late:
         products(act2, weight2, t, outer)
-    for copy in edges2:
+    for copy in edges2_early:
         copy.wait_recv()
     late_row = lax.broadcasted_iota(jnp.int32, (48, 128), 0) % 8 >= 4
     edge_own[...] = jnp.where(late_row, edge_own[...], whole_edges(2))
-    take_past(act2, past2)
+    edge_products(edge_cells(edge_own[...], None), weight2)
+    for t in late:
+        third(t)
+    low_late = send(block.at[pl.ds(2, 2), 0], block.at[pl.ds(2, 2), 4], up)
+    wait_rows(act2, 0, rims2)
     for t in early:
-        products(act2, weight2, t, middle)
         products(act2, weight2, t, outer)
+    past_edges2.wait_recv()
     edge_products(edge_cells(edge_own[...], past_edges(1)), weight2)
-    for t in range(4):
+    for t in early:
         third(t)
-    low_rows = send(block.at[:, 0], block.at[:, 4], up)
+    low_early = send(block.at[pl.ds(0, 2), 0], block.at[pl.ds(0, 2), 4], up)
     total = jnp.zeros((channels, 128), f32)
     for t in range(4):
         for r in range(4):
@@ -392,7 +414,8 @@
         send(edge_out.at[3, pl.ds(0, 16)], edge_side.at[1, 3, pl.ds(0, 16)], left),
         send(edge_out.at[3, pl.ds(0, 16)], edge_corner.at[3, 3], up_left),
     ]
-    low_rows.wait_recv()
+    low_late.wait_recv()
+    low_early.wait_recv()
     for t in range(4):
         masked(block, (t, 4), down_ok)
     for t in range(4):
@@ -457,10 +480,11 @@
     out = pl.pallas_call(
         functools.partial(kernel, GRID_COLUMN_COUNT, grid_rows, groups),
         out_shape=jax.ShapeDtypeStruct((frames, channels, 128), bf16),
-        in_specs=[pl.BlockSpec(memory_space=pltpu.SMEM)] * 2
-        + [pl.BlockSpec(memory_space=pl.ANY)] * 9,
+        in_specs=[pl.BlockSpec(memory_space=pl.ANY)] * 11,
         out_specs=pl.BlockSpec(memory_space=pl.ANY),
         scratch_shapes=[
+            pltpu.SMEM((1, 4), jnp.int32),
+            pltpu.SMEM((1, 2), jnp.int32),
             vmem((4, channels * 4, 128), bf16),
             vmem((channels * 4, 128), f32),
             vmem((4, 4, channels, 128), bf16),
@@ -482,7 +506,7 @@
             vmem((2, 48, 128), bf16),
             vmem((2, 48, 128), bf16),
             vmem((4, channels, 128), bf16),
-            pltpu.SemaphoreType.DMA((12,)),
+            pltpu.SemaphoreType.DMA((14,)),
             pltpu.SemaphoreType.DMA((COPIES,)),
             pltpu.SemaphoreType.DMA((COPIES,)),
             pltpu.SemaphoreType.DMA((4,)),

time: 40.8 us -> 37 us (0.907)
  Pallas kernels: 39.1 us -> 35.3 us
    pallas_call x1, Pallas kernels: 39.1 us -> 35.3 us  [per_device(): pl.pallas_call(functools.partial(kernel, GRID_COLUMN_COUNT, grid_rows, gr...]
where the time goes in v3:
time: 37 us; the launch traced here: 36.9 us
  Pallas kernels  35.3 us (95%)
  local copies, waits for them, and re-layouts  1.54 us (4%)
    pallas_call x1, Pallas kernels, per_device(): pl.pallas_call(functools.partial(kernel, GRID_COLUMN_COUNT, grid_rows, gr...  35.3 us
    unnamed x1, local copies, waits for them, and re-layouts  1.54 us

profile of v3, /device:TPU:1, one launch (start us, length us, event | category | flops | bytes accessed | tf_op | source)
XLA Modules:
  0.0 36.9 jit_solution(8817691973012686110)
XLA Ops:
  0.0 35.3 %shard_map.109 = bf16[4,96,128]{2,1,0:T(8,128)(2,1)} custom-call(s32[1,4]{1,0:T(1,128)} %links_hbm.1, s32[1,2]{1,0:T(1,128)} %extents_hbm.1, bf16[4,384,128]{2,1,0:T(8,128)(2,1)} %bitcast.7, f32[1,96]{1,0:T(1,128)} %bitcast.9, bf16[96,2592]{1,0:T(8,128)(2,1)} %w1_hbm.1, f32[1,96]{1,0:T(1,128)} %bitcast.10, f32[1,96]{1,0:T(1,128)} %bitcast.11, ...), custom_call_target="tpu_custom_call" | custom-call | tf_op jit(solution)/shard_map/pallas_call | solution.py:480
  35.3 1.5 %copy.13 = bf16[1,4,96,128]{3,2,1,0:T(8,128)(2,1)} copy(bf16[1,4,96,128]{3,2,1,0:T(8,128)(2,1)} %bitcast.8) | data formatting | bytes 196608

commit v4 on v3

v4 whole, which is shorter than its diff:
```python
import functools

import jax
import jax.numpy as jnp
from jax import lax
from jax.experimental import pallas as pl
from jax.experimental.pallas import tpu as pltpu
from jax.sharding import PartitionSpec as P

GRID_COLUMN_COUNT = 8
MESH = pl.DeviceIdType.MESH
norm_eps = 1e-06
f32 = jnp.float32
bf16 = jnp.bfloat16

COPIES = 48


def kernel(
    grid_cols,
    grid_rows,
    groups,
    links_hbm,
    extents_hbm,
    x_hbm,
    g1_hbm,
    w1_hbm,
    b1_hbm,
    g2_hbm,
    w2_hbm,
    b2_hbm,
    wd_hbm,
    bd_hbm,
    out_hbm,
    links,
    extents,
    x_raw,
    spread,
    x_rows,
    w_raw,
    wd_raw,
    vec_raw,
    vecs,
    w_conv,
    w_down,
    x_low,
    act1,
    act2,
    block,
    sums,
    edge_sum,
    column_sum,
    pick1,
    pick2,
    edge_own,
    edge_out,
    edge_side,
    edge_corner,
    edge_on,
    edge_past,
    result,
    load_sem,
    send_sem,
    recv_sem,
    store_sem,
):
    channels = vecs.shape[1]
    tile = lax.axis_index("tile")
    group = lax.axis_index("tm")
    grow, gcol = tile // grid_cols, tile % grid_cols
    up, down, left, right = (-1, 0, 0), (1, 0, 0), (0, -1, 0), (0, 1, 0)
    up_left, up_right, down_left, down_right = (-1, -1, 0), (-1, 1, 0), (1, -1, 0), (1, 1, 0)
    later, before = (0, 0, 1), (0, 0, -1)
    around = (up, down, left, right, up_left, up_right, down_left, down_right, later, before)

    def device_at(step):
        row = (grow + step[0] + grid_rows) % grid_rows
        col = (gcol + step[1] + grid_cols) % grid_cols
        return (row * grid_cols + col, (group + step[2] + groups) % groups)

    def is_there(step):
        there = None
        for at, move, size in zip((grow, gcol, group), step, (grid_rows, grid_cols, groups)):
            if move:
                ok = at + move >= 0 if move < 0 else at + move < size
                there = ok if there is None else there & ok
        return there

    there = {step: is_there(step) for step in around}

    barrier = pltpu.get_barrier_semaphore()
    for step in around:

        @pl.when(there[step])
        def _(step=step):
            pl.semaphore_signal(
                barrier, inc=1, device_id=device_at(step), device_id_type=MESH
            )

    loads = []

    def load(src, dst):
        copy = pltpu.make_async_copy(src, dst, load_sem.at[len(loads)])
        copy.start()
        loads.append(copy)
        return copy

    x_loads = {t: load(x_hbm.at[t], x_raw.at[t]) for t in (2, 3, 0, 1)}
    vec_loads = [
        load(ref, vec_raw.at[i]) for i, ref in enumerate((g1_hbm, b1_hbm, g2_hbm, b2_hbm, bd_hbm))
    ]
    scalar_loads = [load(links_hbm, links), load(extents_hbm, extents)]
    w1_load = load(w1_hbm, w_raw.at[0])
    w2_load = load(w2_hbm, w_raw.at[1])
    wd_load = load(wd_hbm, wd_raw)

    sends = []

    def send(src, dst, step):
        i = len(sends)
        copy = pltpu.make_async_remote_copy(
            src_ref=src,
            dst_ref=dst,
            send_sem=send_sem.at[i],
            recv_sem=recv_sem.at[i],
            device_id=device_at(step),
            device_id_type=MESH,
        )
        pl.when(there[step])(copy.start)
        sends.append((copy, there[step]))
        return copy, there[tuple(-move for move in step)]

    def arrive(*copies):
        for copy, ok in copies:
            pl.when(ok)(copy.wait_recv)

    lane = lax.broadcasted_iota(jnp.int32, (channels, 128), 1)
    lane_row = lax.broadcasted_iota(jnp.int32, (1, 128), 1)
    for copy in scalar_loads:
        copy.wait()
    up_ok, down_ok = links[0, 0] >= 0, links[0, 1] >= 0
    left_ok, right_ok = links[0, 2] >= 0, links[0, 3] >= 0
    row_count, col_count = extents[0, 0], extents[0, 1]

    def inside(r):
        cols = jnp.where(r < row_count, col_count, 0)
        return (lane_row < cols).astype(f32)

    def activate(values, gain, r):
        mean_square = jnp.mean(values * values, axis=0, keepdims=True)
        normed = values * lax.rsqrt(mean_square + norm_eps) * gain
        return (normed / (1.0 + jnp.exp(-normed)) * inside(r)).astype(bf16)

    diagonal = lax.broadcasted_iota(jnp.int32, (channels, channels), 0) == lax.broadcasted_iota(
        jnp.int32, (channels, channels), 1
    )

    def spread_vector(i):
        vec_loads[i].wait()
        column = jnp.sum(jnp.where(diagonal, vec_raw[i], 0.0), axis=1, keepdims=True)
        vecs[i] = jnp.broadcast_to(column, (channels, 128))

    def first(t):
        x_loads[t].wait()
        spread[...] = x_raw[t].astype(f32)
        gain = vecs[0]
        for r in range(4):
            values = spread[pl.ds(r, channels, stride=4), :]
            x_rows[t, r] = values.astype(bf16)
            act1[2 + t, 1 + r] = activate(values, gain, r)

    def masked(ref, index, ok):
        ref[index] = jnp.where(ok, ref[index], jnp.zeros_like(ref[index]))

    def send_rows(act, f):
        frames = pl.ds(f, 2)
        copies = [
            send(act.at[frames, 4], act.at[frames, 0], down),
            send(act.at[frames, 1], act.at[frames, 5], up),
        ]
        if act.shape[1] > 6:
            copies.append(send(act.at[frames, 2], act.at[frames, 6], up))
        return copies

    def wait_rows(act, f, copies):
        arrive(*copies[:2])
        for g in (f, f + 1):
            masked(act, (g, 0), up_ok)
            masked(act, (g, 5), down_ok)

    def wait_low_row(act, f, copies):
        arrive(copies[2])
        for g in (f, f + 1):
            masked(act, (g, 6), down_ok)

    def send_past_row(act, row):
        return send(act.at[new_frames, row], act.at[past_frames, row], later)

    def send_past_middle(act):
        return send(act.at[new_frames, pl.ds(2, 2)], act.at[past_frames, pl.ds(2, 2)], later)

    pick_row = lax.broadcasted_iota(jnp.int32, (64, 128), 0)
    pick_lane = lax.broadcasted_iota(jnp.int32, (64, 128), 1)

    def picks(*pairs):
        hit = False
        for row, col in pairs:
            hit = hit | ((pick_row == row) & (pick_lane == col))
        return jnp.where(hit, 1.0, 0.0).astype(bf16)

    def edge_row(t, r):
        return r // 2 * 32 + r % 2 * 8 + t * 2

    def fill_picks(ref, *wanted):
        for i, pairs in enumerate(wanted):
            for t in range(4):
                for r in range(4):
                    at = ((i * 4 + t) * 4 + r) * 128
                    ref[:, at : at + 128] = picks(
                        *[(edge_row(t, r) + row, col) for row, col in pairs]
                    )

    def gather_edges(slot, pick, cells):
        rows = lax.dot_general(
            pick,
            jnp.concatenate(cells, axis=1),
            (((1,), (1,)), ((), ())),
            preferred_element_type=f32,
        )
        edge_out[slot, :, :channels] = rows.astype(bf16)
        edge_out[slot, :, channels:] = jnp.zeros((64, 128 - channels), bf16)

    def gather_edges2(slot, frames):
        cells = [act2[2 + t, 1 + r] for t in frames for r in range(4)]
        gather_edges(slot, pick2[:, frames[0] * 512 : frames[0] * 512 + 1024], cells)
        return send_edges(slot)

    def send_edges(slot):
        whole, upper, lower = (
            edge_out.at[slot],
            edge_out.at[slot, pl.ds(0, 32)],
            edge_out.at[slot, pl.ds(32, 32)],
        )
        copies = [
            send(whole, edge_side.at[0, slot], right),
            send(whole, edge_side.at[1, slot], left),
            send(lower, edge_corner.at[0, slot], down_right),
            send(lower, edge_corner.at[1, slot], down_left),
            send(upper, edge_corner.at[2, slot], up_right),
            send(upper, edge_corner.at[3, slot], up_left),
        ]
        if slot > 0:
            copies += [
                send(lower, edge_corner.at[4, slot], down),
                send(upper, edge_corner.at[5, slot], up),
            ]
        return copies

    def chosen(even, even_ok, odd, odd_ok):
        odd_row = lax.broadcasted_iota(jnp.int32, even.shape, 0) % 2 == 1
        even = jnp.where(even_ok, even, 0.0)
        return jnp.where(odd_row, jnp.where(odd_ok, odd, 0.0), even)

    def whole(value, part):
        value = value.astype(f32)
        return jnp.concatenate(
            [value[16 * part : 16 * part + 16], value[16 * part + 32 : 16 * part + 48]], axis=0
        )

    def above(i, slot, part):
        return edge_corner[i, slot].astype(f32)[16 * part + 8 : 16 * part + 16]

    def below(i, slot, part):
        return edge_corner[i, slot].astype(f32)[16 * part : 16 * part + 16]

    def sides(slot):
        return chosen(
            whole(edge_side[0, slot], 0), left_ok, whole(edge_side[1, slot], 0), right_ok
        )

    def outer_edges(slot):
        upper = chosen(above(0, slot, 0), up_ok & left_ok, above(1, slot, 0), up_ok & right_ok)
        lower = chosen(below(2, slot, 0), down_ok & left_ok, below(3, slot, 0), down_ok & right_ok)
        return jnp.concatenate([upper, sides(slot), lower], axis=0)

    def inner_edges(slot):
        upper = chosen(above(4, slot, 0), up_ok, above(1, slot, 1), up_ok & right_ok)
        middle = chosen(whole(edge_out[slot], 0), True, whole(edge_side[1, slot], 1), right_ok)
        lower = chosen(below(5, slot, 0), down_ok, below(3, slot, 1), down_ok & right_ok)
        return jnp.concatenate([upper, middle, lower], axis=0)

    def edge_cells(own, past):
        first_half = lax.broadcasted_iota(jnp.int32, (8, 128), 0) < 4
        pieces = []
        for row in range(7):
            mine = pltpu.roll(own[8 * row : 8 * row + 8], 4, 0)
            theirs = 0.0
            if past is not None:
                theirs = pltpu.roll(past[8 * row : 8 * row + 8], 4, 0)
            pieces += [jnp.where(first_half, theirs, mine), jnp.where(first_half, mine, 0.0)]
        pieces.append(jnp.zeros((16, 128), f32))
        return jnp.concatenate(pieces, axis=0).T[:channels]

    def patches(act, t, r):
        return jnp.concatenate(
            [act[t + dt, r : r + 3].reshape(3 * channels, 128) for dt in range(3)], axis=0
        )

    def products(act, weight, cells):
        operand = jnp.concatenate([patches(act, t, r) for t, r in cells], axis=1)
        total = jnp.dot(weight[...], operand, preferred_element_type=f32)
        for i, (t, r) in enumerate(cells):
            sums[t, r] = total[:, 128 * i : 128 * i + 128]

    def stacked(cells):
        return jnp.concatenate(
            [
                cells if dt + dr == 0 else pltpu.roll(cells, 128 - (16 * dr + 2 * dt), 1)
                for dt in range(3)
                for dr in range(3)
            ],
            axis=0,
        ).astype(bf16)

    def product(rows, operand):
        return jnp.dot(rows, operand, preferred_element_type=f32)

    def edge_products(cells, weight):
        operand = stacked(cells)
        west = product(weight[:channels], operand)
        east = product(weight[2 * channels :], operand)
        edge_sum[...] = jnp.where(
            lane % 2 == 1, pltpu.roll(west, 1, 1), pltpu.roll(east, 127, 1)
        )

    def column_products(outer_cells, inner_cells, weight):
        both = product(weight[...], stacked(outer_cells))
        west, centre, east = (both[i * channels : (i + 1) * channels] for i in range(3))
        edge_sum[...] = jnp.where(
            lane % 2 == 1, pltpu.roll(west, 1, 1), pltpu.roll(east, 127, 1)
        )
        operand = stacked(inner_cells)
        west = product(weight[:channels], operand)
        east = product(weight[2 * channels :], operand)
        column_sum[...] = centre + east + pltpu.roll(west, 1, 1)

    def convolved(t, r):
        k = 16 * r + 2 * t
        ends = pltpu.roll(edge_sum[...], 128 - (k + 1), 1)
        west = jnp.where(lane == 0, ends, pltpu.roll(sums[t, r, :channels], 1, 1))
        east = jnp.where(lane == 127, ends, pltpu.roll(sums[t, r, 2 * channels :], 127, 1))
        return west + sums[t, r, channels : 2 * channels] + east

    def arrange(raw, taps, step, store):
        value = raw.astype(f32)
        for dc in range(3):
            parts = [
                value[:, (3 * tap + dc) * channels : (3 * tap + dc + 1) * channels]
                for tap in range(taps)
            ]
            store(dc, jnp.concatenate(parts, axis=1).astype(bf16))

    def store_conv(i):
        def put(dc, rows):
            w_conv[i, dc * channels : (dc + 1) * channels] = rows

        return put

    def store_down(dc, rows):
        w_down[dc * channels : (dc + 1) * channels] = rows

    def second(t, rows):
        for r in rows:
            act2[2 + t, 1 + r] = activate(convolved(t, r) + vecs[1], vecs[2], r)

    def third(t):
        for r in range(5):
            residual = x_rows[t, r] if r < 4 else x_low[t]
            total = residual.astype(f32) + (convolved(t, r) + vecs[3])
            ok = inside(r) if r < 4 else low_inside
            block[t, r] = (total * ok).astype(bf16)

    late, early, middle, outer = (2, 3), (0, 1), (1, 2), (0, 3)
    past_frames = pl.ds(0, 2)
    new_frames = pl.ds(4, 2)
    weight1, weight2 = w_conv.at[0], w_conv.at[1]

    def take_past_outer(act, copies):
        arrive(*copies)
        for f in (0, 1):
            for row in (1, 4):
                masked(act, (f, row), group > 0)
        return send_rows(act, 0)

    def take_past_middle(act, copy):
        arrive(copy)
        for f in (0, 1):
            masked(act, (f, slice(2, 4)), group > 0)

    def past_edges(layer, part):
        return jnp.where(group > 0, edge_past[layer, part].astype(f32), 0.0)[:56]

    no_rows = jnp.zeros((8, 128), f32)

    def send_past_edges(layer, parts):
        for i, cells in enumerate(parts):
            edge_on[layer, i] = jnp.concatenate([cells, no_rows], axis=0).astype(bf16)
        some = pl.ds(0, len(parts))
        return send(edge_on.at[layer, some], edge_past.at[layer, some], later)

    spread_vector(0)
    for t in (2, 3, 0, 1):
        first(t)
    fill_picks(pick1, ((0, 127), (1, 0)), ((17, 0),))
    cells = [(t, r) for t in range(4) for r in range(4)]
    gather_edges(
        0, pick1[...], [act1[2 + t, 1 + r] for t, r in cells] + [x_rows[t, r] for t, r in cells]
    )
    pl.semaphore_wait(barrier, sum(there[step].astype(jnp.int32) for step in around))

    outer1 = [send_past_row(act1, 1), send_past_row(act1, 4)]
    edges1 = send_edges(0)
    rows1 = send_rows(act1, 4) + send_rows(act1, 2)
    middle1 = send_past_middle(act1)
    low1 = send(x_rows.at[:, 0], x_low, up)
    w1_load.wait()
    arrange(w_raw[0], 9, 3, store_conv(0))
    for i in range(1, 5):
        spread_vector(i)
    fill_picks(pick2, ((0, 127), (1, 0), (17, 1)))

    for t in late:
        products(act1, weight1, [(t, r) for r in middle])
    arrive(*edges1[:2])
    edge_products(
        edge_cells(jnp.concatenate([no_rows, sides(0), no_rows, no_rows], axis=0), None), weight1
    )
    for t in late:
        second(t, middle)
    middle2 = send_past_middle(act2)
    rims1 = take_past_outer(act1, outer1)
    arrive(*edges1[2:])
    own = outer_edges(0)
    edge_own[0] = own
    past_edges1 = send_past_edges(0, [own])
    wait_rows(act1, 4, rows1[:2])
    wait_rows(act1, 2, rows1[2:])
    for t in late:
        products(act1, weight1, [(t, r) for r in outer])
    edge_products(edge_cells(own, None), weight1)
    for t in late:
        second(t, outer)
    outer2 = [send_past_row(act2, 1), send_past_row(act2, 4)]
    edges2_late = gather_edges2(1, late)
    rows2_late = send_rows(act2, 4)

    take_past_middle(act1, middle1)
    for t in early:
        products(act1, weight1, [(t, r) for r in middle])
    w2_load.wait()
    arrange(w_raw[1], 9, 3, store_conv(1))
    wait_rows(act1, 0, rims1)
    for t in early:
        products(act1, weight1, [(t, r) for r in outer])
    arrive(past_edges1)
    edge_products(edge_cells(edge_own[0], past_edges(0, 0)), weight1)
    for t in early:
        second(t, range(4))
    edges2_early = gather_edges2(2, early)
    rows2_early = send_rows(act2, 2)
    take_past_middle(act2, middle2)
    rims2 = take_past_outer(act2, outer2)
    arrive(*edges2_late)
    edge_own[0] = outer_edges(1)
    edge_own[1] = inner_edges(1)
    past_edges2 = send_past_edges(1, [edge_own[0], edge_own[1]])
    wd_load.wait()
    arrange(wd_raw[...], 3, 1, store_down)

    arrive(low1)
    for t in range(4):
        masked(x_low, t, down_ok)
    low_inside = (lane_row < jnp.where(down_ok, col_count, 0)).astype(f32)
    for t in range(4):
        products(act2, weight2, [(t, r) for r in middle])
    wait_rows(act2, 4, rows2_late)
    wait_rows(act2, 2, rows2_early)
    for t in late:
        products(act2, weight2, [(t, r) for r in outer])
    wait_low_row(act2, 4, rows2_late)
    wait_low_row(act2, 2, rows2_early)
    products(act2, weight2, [(t, 4) for t in late])
    arrive(*edges2_early)
    late_row = lax.broadcasted_iota(jnp.int32, (56, 128), 0) % 8 >= 4
    outer_own = jnp.where(late_row, edge_own[0], outer_edges(2))
    inner_own = jnp.where(late_row, edge_own[1], inner_edges(2))
    arrive(past_edges2)
    column_products(
        edge_cells(outer_own, past_edges(1, 0)), edge_cells(inner_own, past_edges(1, 1)), weight2
    )
    for t in late:
        third(t)
    wait_rows(act2, 0, rims2)
    for t in early:
        products(act2, weight2, [(t, r) for r in outer])
    wait_low_row(act2, 0, rims2)
    products(act2, weight2, [(t, 4) for t in early])
    for t in early:
        third(t)
    x_column = [edge_side[1, 0].astype(f32)[16:32], edge_side[1, 0].astype(f32)[48:64]]
    x_column = [x_column[r // 2][8 * (r % 2) : 8 * (r % 2) + 8] for r in range(4)]
    x_column.append(below(3, 0, 1)[:8])
    x_column = sum([[rows, no_rows] for rows in x_column], []) + [jnp.zeros((48, 128), f32)]
    slab_row = lane // 16
    row_inside = ((slab_row < 4) & (slab_row < row_count)) | ((slab_row == 4) & down_ok)
    cells = jnp.concatenate(x_column, axis=0).T[:channels] + (column_sum[...] + vecs[3])
    cells = jnp.where(row_inside & right_ok, cells, 0.0)
    for t in range(4):
        operand = jnp.concatenate(
            [block[t, 2 * i : 2 * i + 3].reshape(3 * channels, 128) for i in range(2)], axis=1
        )
        total = product(w_down[...], operand)
        for i in range(2):
            sums[t, i] = total[:, 128 * i : 128 * i + 128]
    operand = jnp.concatenate(
        [cells, pltpu.roll(cells, 112, 1), pltpu.roll(cells, 96, 1)], axis=0
    ).astype(bf16)
    east = product(w_down[2 * channels :], operand)
    picked = (
        lax.broadcasted_iota(jnp.int32, (256, 128), 0)
        == 2 * lax.broadcasted_iota(jnp.int32, (256, 128), 1)
    ).astype(f32).astype(bf16)
    col_limit = jnp.where(right_ok, 1024, col_count)
    stores = []
    for t in range(4):
        halves = []
        for i in range(2):
            row_limit = jnp.where(down_ok, 1024, row_count)
            limit = jnp.where(2 * i + 2 <= row_limit, col_limit, 0)
            keep = (lane_row + 2 <= limit).astype(f32)
            ends = pltpu.roll(east, 126 - (32 * i + 2 * t + 1), 1)
            total = (
                sums[t, i, :channels]
                + pltpu.roll(sums[t, i, channels : 2 * channels], 127, 1)
                + jnp.where(lane == 126, ends, pltpu.roll(sums[t, i, 2 * channels :], 126, 1))
            )
            halves.append(((total + vecs[4]) * keep).astype(bf16))
        result[t] = jnp.dot(
            jnp.concatenate(halves, axis=1), picked, preferred_element_type=f32
        ).astype(bf16)
        copy = pltpu.make_async_copy(result.at[t], out_hbm.at[t], store_sem.at[t])
        copy.start()
        stores.append(copy)
    for copy, ok in sends:
        pl.when(ok)(copy.wait_send)
    for copy in stores:
        copy.wait()


def per_device(grid_rows, groups, video, links, extents, g1, w1, b1, g2, w2, b2, wd, bd):
    _, frames, channels, slab_rows, slab_cols = video.shape
    x = video.reshape(frames, channels * slab_rows, slab_cols)
    vectors = [v.reshape(1, channels) for v in (g1, b1, g2, b2, bd)]
    g1, b1, g2, b2, bd = vectors
    vmem = pltpu.VMEM
    out = pl.pallas_call(
        functools.partial(kernel, GRID_COLUMN_COUNT, grid_rows, groups),
        out_shape=jax.ShapeDtypeStruct((frames, channels, 128), bf16),
        in_specs=[pl.BlockSpec(memory_space=pl.ANY)] * 11,
        out_specs=pl.BlockSpec(memory_space=pl.ANY),
        scratch_shapes=[
            pltpu.SMEM((1, 4), jnp.int32),
            pltpu.SMEM((1, 2), jnp.int32),
            vmem((4, channels * 4, 128), bf16),
            vmem((channels * 4, 128), f32),
            vmem((4, 4, channels, 128), bf16),
            vmem((2, channels, 27 * channels), bf16),
            vmem((channels, 9 * channels), bf16),
            vmem((5, 1, channels), f32),
            vmem((5, channels, 128), f32),
            vmem((2, 3 * channels, 9 * channels), bf16),
            vmem((3 * channels, 3 * channels), bf16),
            vmem((4, channels, 128), bf16),
            vmem((6, 6, channels, 128), bf16),
            vmem((6, 7, channels, 128), bf16),
            vmem((4, 5, channels, 128), bf16),
            vmem((4, 5, 3 * channels, 128), f32),
            vmem((channels, 128), f32),
            vmem((channels, 128), f32),
            vmem((64, 32 * 128), bf16),
            vmem((64, 16 * 128), bf16),
            vmem((2, 56, 128), f32),
            vmem((3, 64, 128), bf16),
            vmem((2, 3, 64, 128), bf16),
            vmem((6, 3, 32, 128), bf16),
            vmem((2, 2, 64, 128), bf16),
            vmem((2, 2, 64, 128), bf16),
            vmem((4, channels, 128), bf16),
            pltpu.SemaphoreType.DMA((14,)),
            pltpu.SemaphoreType.DMA((COPIES,)),
            pltpu.SemaphoreType.DMA((COPIES,)),
            pltpu.SemaphoreType.DMA((4,)),
        ],
        compiler_params=pltpu.CompilerParams(
            collective_id=0, has_side_effects=True, vmem_limit_bytes=60 * 2**20
        ),
    )(links, extents, x, g1, w1, b1, g2, w2, b2, wd, bd)
    return out[None]


def solution(mesh):
    placed = (P("tile", "tm", None, None, None), P("tile", None), P("tile", None)) + (P(),) * 8
    return jax.shard_map(
        functools.partial(
            per_device, mesh.shape["tile"] // GRID_COLUMN_COUNT, mesh.shape["tm"]
        ),
        mesh=mesh,
        in_specs=placed,
        out_specs=P("tile", "tm", None, None),
        check_vma=False,
    )
```

time: 37 us -> 28.5 us (0.77)
  the two profiles are of different devices: /device:TPU:1 before, /device:TPU:124 now
where the time goes in v4:
time: 28.5 us; the launch traced here: 28.4 us
  Pallas kernels  26.8 us (94%)
  local copies, waits for them, and re-layouts  1.54 us (5%)
    pallas_call x1, Pallas kernels, per_device(): pl.pallas_call(functools.partial(kernel, GRID_COLUMN_COUNT, grid_rows, gr...  26.8 us
    unnamed x1, local copies, waits for them, and re-layouts  1.54 us

profile of v4, /device:TPU:124, one launch (start us, length us, event | category | flops | bytes accessed | tf_op | source)
XLA Modules:
  0.0 28.4 jit_solution(14487231043693730541)
XLA Ops:
  0.0 26.8 %shard_map.109 = bf16[4,96,128]{2,1,0:T(8,128)(2,1)} custom-call(s32[1,4]{1,0:T(1,128)} %links_hbm.1, s32[1,2]{1,0:T(1,128)} %extents_hbm.1, bf16[4,384,128]{2,1,0:T(8,128)(2,1)} %bitcast.7, f32[1,96]{1,0:T(1,128)} %bitcast.9, bf16[96,2592]{1,0:T(8,128)(2,1)} %w1_hbm.1, f32[1,96]{1,0:T(1,128)} %bitcast.10, f32[1,96]{1,0:T(1,128)} %bitcast.11, ...), custom_call_target="tpu_custom_call" | custom-call | tf_op jit(solution)/shard_map/pallas_call | solution.py:566
  26.8 1.5 %copy.13 = bf16[1,4,96,128]{3,2,1,0:T(8,128)(2,1)} copy(bf16[1,4,96,128]{3,2,1,0:T(8,128)(2,1)} %bitcast.8) | data formatting | bytes 196608

commit v5 on v4

--- a/solution.py
+++ b/solution.py
@@ -13,7 +13,7 @@
 f32 = jnp.float32
 bf16 = jnp.bfloat16
 
-COPIES = 48
+COPIES = 64
 
 
 def kernel(
@@ -42,6 +42,7 @@
     vec_raw,
     vecs,
     w_conv,
+    w_edge,
     w_down,
     x_low,
     act1,
@@ -58,6 +59,8 @@
     edge_corner,
     edge_on,
     edge_past,
+    edge_low_on,
+    edge_low_past,
     result,
     load_sem,
     send_sem,
@@ -172,20 +175,28 @@
     def masked(ref, index, ok):
         ref[index] = jnp.where(ok, ref[index], jnp.zeros_like(ref[index]))
 
-    def send_rows(act, f):
+    def send_rows_up(act, f):
         frames = pl.ds(f, 2)
-        copies = [
-            send(act.at[frames, 4], act.at[frames, 0], down),
-            send(act.at[frames, 1], act.at[frames, 5], up),
-        ]
+        copies = [send(act.at[frames, 1], act.at[frames, 5], up)]
         if act.shape[1] > 6:
             copies.append(send(act.at[frames, 2], act.at[frames, 6], up))
         return copies
 
-    def wait_rows(act, f, copies):
-        arrive(*copies[:2])
+    def send_rows_down(act, f):
+        frames = pl.ds(f, 2)
+        return send(act.at[frames, 4], act.at[frames, 0], down)
+
+    def send_rows(act, f):
+        return [send_rows_down(act, f)] + send_rows_up(act, f)
+
+    def wait_upper(act, f, copies):
+        arrive(copies[0])
         for g in (f, f + 1):
             masked(act, (g, 0), up_ok)
+
+    def wait_lower(act, f, copies):
+        arrive(copies[1])
+        for g in (f, f + 1):
             masked(act, (g, 5), down_ok)
 
     def wait_low_row(act, f, copies):
@@ -230,10 +241,30 @@
         edge_out[slot, :, :channels] = rows.astype(bf16)
         edge_out[slot, :, channels:] = jnp.zeros((64, 128 - channels), bf16)
 
-    def gather_edges2(slot, frames):
-        cells = [act2[2 + t, 1 + r] for t in frames for r in range(4)]
-        gather_edges(slot, pick2[:, frames[0] * 512 : frames[0] * 512 + 1024], cells)
-        return send_edges(slot)
+    def gather_edges2(slot, frames, half):
+        mine = pl.ds(32 * half, 32)
+        cells = [act2[2 + t, 1 + r] for t in frames for r in (2 * half, 2 * half + 1)]
+        pick = jnp.concatenate(
+            [pick2[mine, t * 512 + half * 256 : t * 512 + half * 256 + 256] for t in frames],
+            axis=1,
+        )
+        rows = lax.dot_general(
+            pick,
+            jnp.concatenate(cells, axis=1),
+            (((1,), (1,)), ((), ())),
+            preferred_element_type=f32,
+        )
+        edge_out[slot, mine, :channels] = rows.astype(bf16)
+        edge_out[slot, mine, channels:] = jnp.zeros((32, 128 - channels), bf16)
+        part = edge_out.at[slot, mine]
+        first, steps = (
+            (2, (up_right, up_left, up)) if half == 0 else (0, (down_right, down_left, down))
+        )
+        slots = (first, first + 1, 5 if half == 0 else 4)
+        return [
+            send(part, edge_side.at[0, slot, mine], right),
+            send(part, edge_side.at[1, slot, mine], left),
+        ] + [send(part, edge_corner.at[i, slot], step) for i, step in zip(slots, steps)]
 
     def send_edges(slot):
         whole, upper, lower = (
@@ -241,7 +272,7 @@
             edge_out.at[slot, pl.ds(0, 32)],
             edge_out.at[slot, pl.ds(32, 32)],
         )
-        copies = [
+        return [
             send(whole, edge_side.at[0, slot], right),
             send(whole, edge_side.at[1, slot], left),
             send(lower, edge_corner.at[0, slot], down_right),
@@ -249,12 +280,6 @@
             send(upper, edge_corner.at[2, slot], up_right),
             send(upper, edge_corner.at[3, slot], up_left),
         ]
-        if slot > 0:
-            copies += [
-                send(lower, edge_corner.at[4, slot], down),
-                send(upper, edge_corner.at[5, slot], up),
-            ]
-        return copies
 
     def chosen(even, even_ok, odd, odd_ok):
         odd_row = lax.broadcasted_iota(jnp.int32, even.shape, 0) % 2 == 1
@@ -278,10 +303,15 @@
             whole(edge_side[0, slot], 0), left_ok, whole(edge_side[1, slot], 0), right_ok
         )
 
+    def upper_edges(slot):
+        upper = chosen(above(0, slot, 0), up_ok & left_ok, above(1, slot, 0), up_ok & right_ok)
+        return jnp.concatenate([upper, sides(slot)], axis=0)
+
+    def lower_edges(slot):
+        return chosen(below(2, slot, 0), down_ok & left_ok, below(3, slot, 0), down_ok & right_ok)
+
     def outer_edges(slot):
-        upper = chosen(above(0, slot, 0), up_ok & left_ok, above(1, slot, 0), up_ok & right_ok)
-        lower = chosen(below(2, slot, 0), down_ok & left_ok, below(3, slot, 0), down_ok & right_ok)
-        return jnp.concatenate([upper, sides(slot), lower], axis=0)
+        return jnp.concatenate([upper_edges(slot), lower_edges(slot)], axis=0)
 
     def inner_edges(slot):
         upper = chosen(above(4, slot, 0), up_ok, above(1, slot, 1), up_ok & right_ok)
@@ -299,7 +329,7 @@
                 theirs = pltpu.roll(past[8 * row : 8 * row + 8], 4, 0)
             pieces += [jnp.where(first_half, theirs, mine), jnp.where(first_half, mine, 0.0)]
         pieces.append(jnp.zeros((16, 128), f32))
-        return jnp.concatenate(pieces, axis=0).T[:channels]
+        return jnp.concatenate(pieces, axis=0)
 
     def patches(act, t, r):
         return jnp.concatenate(
@@ -313,35 +343,45 @@
             sums[t, r] = total[:, 128 * i : 128 * i + 128]
 
     def stacked(cells):
+        moved = [
+            (cells if dt == 0 else pltpu.roll(cells, 128 - 2 * dt, 0)).astype(bf16)
+            for dt in range(3)
+        ]
+        rest = jnp.zeros((48, 128), bf16)
         return jnp.concatenate(
             [
-                cells if dt + dr == 0 else pltpu.roll(cells, 128 - (16 * dr + 2 * dt), 1)
+                jnp.concatenate([moved[dt][16 * dr : 16 * dr + 80], rest], axis=0)
                 for dt in range(3)
                 for dr in range(3)
             ],
-            axis=0,
-        ).astype(bf16)
+            axis=1,
+        )
+
+    def edge_product(rows, operand):
+        return lax.dot_general(
+            rows, operand, (((1,), (1,)), ((), ())), preferred_element_type=f32
+        )
 
     def product(rows, operand):
         return jnp.dot(rows, operand, preferred_element_type=f32)
 
     def edge_products(cells, weight):
         operand = stacked(cells)
-        west = product(weight[:channels], operand)
-        east = product(weight[2 * channels :], operand)
+        west = edge_product(weight[:channels], operand)
+        east = edge_product(weight[2 * channels :], operand)
         edge_sum[...] = jnp.where(
             lane % 2 == 1, pltpu.roll(west, 1, 1), pltpu.roll(east, 127, 1)
         )
 
     def column_products(outer_cells, inner_cells, weight):
-        both = product(weight[...], stacked(outer_cells))
+        both = edge_product(weight[...], stacked(outer_cells))
         west, centre, east = (both[i * channels : (i + 1) * channels] for i in range(3))
         edge_sum[...] = jnp.where(
             lane % 2 == 1, pltpu.roll(west, 1, 1), pltpu.roll(east, 127, 1)
         )
         operand = stacked(inner_cells)
-        west = product(weight[:channels], operand)
-        east = product(weight[2 * channels :], operand)
+        west = edge_product(weight[:channels], operand)
+        east = edge_product(weight[2 * channels :], operand)
         column_sum[...] = centre + east + pltpu.roll(west, 1, 1)
 
     def convolved(t, r):
@@ -358,16 +398,22 @@
                 value[:, (3 * tap + dc) * channels : (3 * tap + dc + 1) * channels]
                 for tap in range(taps)
             ]
-            store(dc, jnp.concatenate(parts, axis=1).astype(bf16))
+            store(dc, parts)
 
     def store_conv(i):
-        def put(dc, rows):
-            w_conv[i, dc * channels : (dc + 1) * channels] = rows
+        def put(dc, parts):
+            rows = slice(dc * channels, (dc + 1) * channels)
+            w_conv[i, rows] = jnp.concatenate(parts, axis=1).astype(bf16)
+            pad = jnp.zeros((channels, 128 - channels), f32)
+            for tap, part in enumerate(parts):
+                w_edge[i, rows, tap * 128 : tap * 128 + 128] = jnp.concatenate(
+                    [part, pad], axis=1
+                ).astype(bf16)
 
         return put
 
-    def store_down(dc, rows):
-        w_down[dc * channels : (dc + 1) * channels] = rows
+    def store_down(dc, parts):
+        w_down[dc * channels : (dc + 1) * channels] = jnp.concatenate(parts, axis=1).astype(bf16)
 
     def second(t, rows):
         for r in rows:
@@ -384,13 +430,15 @@
     past_frames = pl.ds(0, 2)
     new_frames = pl.ds(4, 2)
     weight1, weight2 = w_conv.at[0], w_conv.at[1]
-
-    def take_past_outer(act, copies):
-        arrive(*copies)
+    edge1, edge2 = w_edge.at[0], w_edge.at[1]
+
+    def take_past_row(act, copy, row):
+        arrive(copy)
         for f in (0, 1):
-            for row in (1, 4):
-                masked(act, (f, row), group > 0)
-        return send_rows(act, 0)
+            masked(act, (f, row), group > 0)
+        if row == 1:
+            return send(act.at[past_frames, 1], act.at[past_frames, 5], up)
+        return send(act.at[past_frames, 4], act.at[past_frames, 0], down)
 
     def take_past_middle(act, copy):
         arrive(copy)
@@ -404,9 +452,22 @@
 
     def send_past_edges(layer, parts):
         for i, cells in enumerate(parts):
-            edge_on[layer, i] = jnp.concatenate([cells, no_rows], axis=0).astype(bf16)
+            edge_on[layer, i] = jnp.concatenate([cells[:40], no_rows], axis=0).astype(bf16)
         some = pl.ds(0, len(parts))
         return send(edge_on.at[layer, some], edge_past.at[layer, some], later)
+
+    def send_past_low(layer, parts):
+        for i, cells in enumerate(parts):
+            edge_low_on[layer, i] = cells.astype(bf16)
+        some = pl.ds(0, len(parts))
+        return send(edge_low_on.at[layer, some], edge_low_past.at[layer, some], later)
+
+    def past_edges(layer, part, low=True):
+        upper = jnp.where(group > 0, edge_past[layer, part].astype(f32)[:40], 0.0)
+        if not low:
+            return jnp.concatenate([upper, no_rows, no_rows], axis=0)
+        lower = jnp.where(group > 0, edge_low_past[layer, part].astype(f32), 0.0)
+        return jnp.concatenate([upper, lower], axis=0)
 
     spread_vector(0)
     for t in (2, 3, 0, 1):
@@ -431,49 +492,76 @@
 
     for t in late:
         products(act1, weight1, [(t, r) for r in middle])
-    arrive(*edges1[:2])
-    edge_products(
-        edge_cells(jnp.concatenate([no_rows, sides(0), no_rows, no_rows], axis=0), None), weight1
-    )
+    arrive(*edges1[:4])
+    upper = upper_edges(0)
+    edge_own[0, :40] = upper
+    past_edges1 = send_past_edges(0, [upper])
+    edge_products(edge_cells(jnp.concatenate([upper, no_rows, no_rows], axis=0), None), edge1)
     for t in late:
         second(t, middle)
     middle2 = send_past_middle(act2)
-    rims1 = take_past_outer(act1, outer1)
-    arrive(*edges1[2:])
-    own = outer_edges(0)
-    edge_own[0] = own
-    past_edges1 = send_past_edges(0, [own])
-    wait_rows(act1, 4, rows1[:2])
-    wait_rows(act1, 2, rows1[2:])
+    rims1_low = take_past_row(act1, outer1[0], 1)
+    rims1_high = take_past_row(act1, outer1[1], 4)
+    wait_upper(act1, 4, rows1[:2])
+    wait_upper(act1, 2, rows1[2:])
+    products(act1, weight1, [(t, 0) for t in late])
     for t in late:
-        products(act1, weight1, [(t, r) for r in outer])
-    edge_products(edge_cells(own, None), weight1)
+        second(t, (0,))
+    outer2 = [send_past_row(act2, 1)]
+    edges2_late = gather_edges2(1, late, 0)
+    rows2_late_up = send_rows_up(act2, 4)
+    arrive(*edges1[4:])
+    low = lower_edges(0)
+    edge_own[0, 40:] = low
+    past_low1 = send_past_low(0, [low])
+    edge_products(edge_cells(edge_own[0], None), edge1)
+    wait_lower(act1, 4, rows1[:2])
+    wait_lower(act1, 2, rows1[2:])
+    products(act1, weight1, [(t, 3) for t in late])
     for t in late:
-        second(t, outer)
-    outer2 = [send_past_row(act2, 1), send_past_row(act2, 4)]
-    edges2_late = gather_edges2(1, late)
-    rows2_late = send_rows(act2, 4)
+        second(t, (3,))
+    outer2.append(send_past_row(act2, 4))
+    edges2_late += gather_edges2(1, late, 1)
+    rows2_late = [send_rows_down(act2, 4)] + rows2_late_up
 
     take_past_middle(act1, middle1)
     for t in early:
         products(act1, weight1, [(t, r) for r in middle])
+    arrive(past_edges1)
+    edge_products(edge_cells(edge_own[0], past_edges(0, 0, False)), edge1)
+    for t in early:
+        second(t, middle)
     w2_load.wait()
     arrange(w_raw[1], 9, 3, store_conv(1))
-    wait_rows(act1, 0, rims1)
+    wait_upper(act1, 0, [rims1_high])
+    products(act1, weight1, [(t, 0) for t in early])
     for t in early:
-        products(act1, weight1, [(t, r) for r in outer])
-    arrive(past_edges1)
-    edge_products(edge_cells(edge_own[0], past_edges(0, 0)), weight1)
+        second(t, (0,))
+    edges2_early = gather_edges2(2, early, 0)
+    rows2_early_up = send_rows_up(act2, 2)
+    arrive(past_low1)
+    edge_products(edge_cells(edge_own[0], past_edges(0, 0)), edge1)
+    wait_lower(act1, 0, [None, rims1_low])
+    products(act1, weight1, [(t, 3) for t in early])
     for t in early:
-        second(t, range(4))
-    edges2_early = gather_edges2(2, early)
-    rows2_early = send_rows(act2, 2)
-    take_past_middle(act2, middle2)
-    rims2 = take_past_outer(act2, outer2)
+        second(t, (3,))
+    edges2_early += gather_edges2(2, early, 1)
+    rows2_early = [send_rows_down(act2, 2)] + rows2_early_up
     arrive(*edges2_late)
     edge_own[0] = outer_edges(1)
     edge_own[1] = inner_edges(1)
-    past_edges2 = send_past_edges(1, [edge_own[0], edge_own[1]])
+    past_edges2 = [
+        send_past_edges(1, [edge_own[0], edge_own[1]]),
+        send_past_low(1, [edge_own[0, 40:], edge_own[1, 40:]]),
+    ]
+    for t in late:
+        products(act2, weight2, [(t, r) for r in middle])
+    take_past_middle(act2, middle2)
+    low_row = send(act2.at[past_frames, 2], act2.at[past_frames, 6], up)
+    rims2 = [None, take_past_row(act2, outer2[0], 1), low_row]
+    rims2[0] = take_past_row(act2, outer2[1], 4)
+    for t in early:
+        products(act2, weight2, [(t, r) for r in middle])
     wd_load.wait()
     arrange(wd_raw[...], 3, 1, store_down)
 
@@ -481,32 +569,14 @@
     for t in range(4):
         masked(x_low, t, down_ok)
     low_inside = (lane_row < jnp.where(down_ok, col_count, 0)).astype(f32)
-    for t in range(4):
-        products(act2, weight2, [(t, r) for r in middle])
-    wait_rows(act2, 4, rows2_late)
-    wait_rows(act2, 2, rows2_early)
-    for t in late:
-        products(act2, weight2, [(t, r) for r in outer])
-    wait_low_row(act2, 4, rows2_late)
-    wait_low_row(act2, 2, rows2_early)
-    products(act2, weight2, [(t, 4) for t in late])
     arrive(*edges2_early)
     late_row = lax.broadcasted_iota(jnp.int32, (56, 128), 0) % 8 >= 4
     outer_own = jnp.where(late_row, edge_own[0], outer_edges(2))
     inner_own = jnp.where(late_row, edge_own[1], inner_edges(2))
-    arrive(past_edges2)
+    arrive(*past_edges2)
     column_products(
-        edge_cells(outer_own, past_edges(1, 0)), edge_cells(inner_own, past_edges(1, 1)), weight2
+        edge_cells(outer_own, past_edges(1, 0)), edge_cells(inner_own, past_edges(1, 1)), edge2
     )
-    for t in late:
-        third(t)
-    wait_rows(act2, 0, rims2)
-    for t in early:
-        products(act2, weight2, [(t, r) for r in outer])
-    wait_low_row(act2, 0, rims2)
-    products(act2, weight2, [(t, 4) for t in early])
-    for t in early:
-        third(t)
     x_column = [edge_side[1, 0].astype(f32)[16:32], edge_side[1, 0].astype(f32)[48:64]]
     x_column = [x_column[r // 2][8 * (r % 2) : 8 * (r % 2) + 8] for r in range(4)]
     x_column.append(below(3, 0, 1)[:8])
@@ -515,42 +585,63 @@
     row_inside = ((slab_row < 4) & (slab_row < row_count)) | ((slab_row == 4) & down_ok)
     cells = jnp.concatenate(x_column, axis=0).T[:channels] + (column_sum[...] + vecs[3])
     cells = jnp.where(row_inside & right_ok, cells, 0.0)
-    for t in range(4):
-        operand = jnp.concatenate(
-            [block[t, 2 * i : 2 * i + 3].reshape(3 * channels, 128) for i in range(2)], axis=1
-        )
-        total = product(w_down[...], operand)
-        for i in range(2):
-            sums[t, i] = total[:, 128 * i : 128 * i + 128]
     operand = jnp.concatenate(
         [cells, pltpu.roll(cells, 112, 1), pltpu.roll(cells, 96, 1)], axis=0
     ).astype(bf16)
-    east = product(w_down[2 * channels :], operand)
+    column_sum[...] = product(w_down[2 * channels :], operand)
     picked = (
         lax.broadcasted_iota(jnp.int32, (256, 128), 0)
         == 2 * lax.broadcasted_iota(jnp.int32, (256, 128), 1)
     ).astype(f32).astype(bf16)
     col_limit = jnp.where(right_ok, 1024, col_count)
+    row_limit = jnp.where(down_ok, 1024, row_count)
     stores = []
-    for t in range(4):
-        halves = []
-        for i in range(2):
-            row_limit = jnp.where(down_ok, 1024, row_count)
-            limit = jnp.where(2 * i + 2 <= row_limit, col_limit, 0)
-            keep = (lane_row + 2 <= limit).astype(f32)
-            ends = pltpu.roll(east, 126 - (32 * i + 2 * t + 1), 1)
-            total = (
-                sums[t, i, :channels]
-                + pltpu.roll(sums[t, i, channels : 2 * channels], 127, 1)
-                + jnp.where(lane == 126, ends, pltpu.roll(sums[t, i, 2 * channels :], 126, 1))
+
+    def encode(frames):
+        for t in frames:
+            operand = jnp.concatenate(
+                [block[t, 2 * i : 2 * i + 3].reshape(3 * channels, 128) for i in range(2)], axis=1
             )
-            halves.append(((total + vecs[4]) * keep).astype(bf16))
-        result[t] = jnp.dot(
-            jnp.concatenate(halves, axis=1), picked, preferred_element_type=f32
-        ).astype(bf16)
-        copy = pltpu.make_async_copy(result.at[t], out_hbm.at[t], store_sem.at[t])
-        copy.start()
-        stores.append(copy)
+            total = product(w_down[...], operand)
+            for i in range(2):
+                sums[t, i] = total[:, 128 * i : 128 * i + 128]
+        for t in frames:
+            halves = []
+            for i in range(2):
+                limit = jnp.where(2 * i + 2 <= row_limit, col_limit, 0)
+                keep = (lane_row + 2 <= limit).astype(f32)
+                ends = pltpu.roll(column_sum[...], 126 - (32 * i + 2 * t + 1), 1)
+                total = (
+                    sums[t, i, :channels]
+                    + pltpu.roll(sums[t, i, channels : 2 * channels], 127, 1)
+                    + jnp.where(lane == 126, ends, pltpu.roll(sums[t, i, 2 * channels :], 126, 1))
+                )
+                halves.append(((total + vecs[4]) * keep).astype(bf16))
+            result[t] = product(jnp.concatenate(halves, axis=1), picked).astype(bf16)
+            copy = pltpu.make_async_copy(result.at[t], out_hbm.at[t], store_sem.at[t])
+            copy.start()
+            stores.append(copy)
+
+    for f, copies in ((4, rows2_late), (2, rows2_early)):
+        wait_upper(act2, f, copies)
+        wait_lower(act2, f, copies)
+    for t in late:
+        products(act2, weight2, [(t, r) for r in outer])
+    wait_low_row(act2, 4, rows2_late)
+    wait_low_row(act2, 2, rows2_early)
+    products(act2, weight2, [(t, 4) for t in late])
+    for t in late:
+        third(t)
+    encode(late)
+    wait_upper(act2, 0, rims2)
+    wait_lower(act2, 0, rims2)
+    for t in early:
+        products(act2, weight2, [(t, r) for r in outer])
+    wait_low_row(act2, 0, rims2)
+    products(act2, weight2, [(t, 4) for t in early])
+    for t in early:
+        third(t)
+    encode(early)
     for copy, ok in sends:
         pl.when(ok)(copy.wait_send)
     for copy in stores:
@@ -579,6 +670,7 @@
             vmem((5, 1, channels), f32),
             vmem((5, channels, 128), f32),
             vmem((2, 3 * channels, 9 * channels), bf16),
+            vmem((2, 3 * channels, 9 * 128), bf16),
             vmem((3 * channels, 3 * channels), bf16),
             vmem((4, channels, 128), bf16),
             vmem((6, 6, channels, 128), bf16),
@@ -593,8 +685,10 @@
             vmem((3, 64, 128), bf16),
             vmem((2, 3, 64, 128), bf16),
             vmem((6, 3, 32, 128), bf16),
-            vmem((2, 2, 64, 128), bf16),
-            vmem((2, 2, 64, 128), bf16),
+            vmem((2, 2, 48, 128), bf16),
+            vmem((2, 2, 48, 128), bf16),
+            vmem((2, 2, 16, 128), bf16),
+            vmem((2, 2, 16, 128), bf16),
             vmem((4, channels, 128), bf16),
             pltpu.SemaphoreType.DMA((14,)),
             pltpu.SemaphoreType.DMA((COPIES,)),

time: 28.5 us -> 27.9 us (0.979)
  the two profiles are of different devices: /device:TPU:124 before, /device:TPU:1 now
where the time goes in v5:
time: 27.9 us; the launch traced here: 27.8 us
  Pallas kernels  26.2 us (94%)
  local copies, waits for them, and re-layouts  1.54 us (6%)
    pallas_call x1, Pallas kernels, per_device(): pl.pallas_call(functools.partial(kernel, GRID_COLUMN_COUNT, grid_rows, gr...  26.2 us
    unnamed x1, local copies, waits for them, and re-layouts  1.54 us

profile of v5, /device:TPU:1, one launch (start us, length us, event | category | flops | bytes accessed | tf_op | source)
XLA Modules:
  0.0 27.8 jit_solution(10036293886962286167)
XLA Ops:
  0.0 26.2 %shard_map.109 = bf16[4,96,128]{2,1,0:T(8,128)(2,1)} custom-call(s32[1,4]{1,0:T(1,128)} %links_hbm.1, s32[1,2]{1,0:T(1,128)} %extents_hbm.1, bf16[4,384,128]{2,1,0:T(8,128)(2,1)} %bitcast.7, f32[1,96]{1,0:T(1,128)} %bitcast.9, bf16[96,2592]{1,0:T(8,128)(2,1)} %w1_hbm.1, f32[1,96]{1,0:T(1,128)} %bitcast.10, f32[1,96]{1,0:T(1,128)} %bitcast.11, ...), custom_call_target="tpu_custom_call" | custom-call | tf_op jit(solution)/shard_map/pallas_call | solution.py:657
  26.2 1.5 %copy.13 = bf16[1,4,96,128]{3,2,1,0:T(8,128)(2,1)} copy(bf16[1,4,96,128]{3,2,1,0:T(8,128)(2,1)} %bitcast.8) | data formatting | bytes 196608

commit v6 on v5

--- a/solution.py
+++ b/solution.py
@@ -479,8 +479,8 @@
     )
     pl.semaphore_wait(barrier, sum(there[step].astype(jnp.int32) for step in around))
 
+    edges1 = send_edges(0)
     outer1 = [send_past_row(act1, 1), send_past_row(act1, 4)]
-    edges1 = send_edges(0)
     rows1 = send_rows(act1, 4) + send_rows(act1, 2)
     middle1 = send_past_middle(act1)
     low1 = send(x_rows.at[:, 0], x_low, up)
@@ -547,6 +547,10 @@
         second(t, (3,))
     edges2_early += gather_edges2(2, early, 1)
     rows2_early = [send_rows_down(act2, 2)] + rows2_early_up
+    rims2 = [None, take_past_row(act2, outer2[0], 1), None]
+    take_past_middle(act2, middle2)
+    rims2[2] = send(act2.at[past_frames, 2], act2.at[past_frames, 6], up)
+    rims2[0] = take_past_row(act2, outer2[1], 4)
     arrive(*edges2_late)
     edge_own[0] = outer_edges(1)
     edge_own[1] = inner_edges(1)
@@ -556,10 +560,6 @@
     ]
     for t in late:
         products(act2, weight2, [(t, r) for r in middle])
-    take_past_middle(act2, middle2)
-    low_row = send(act2.at[past_frames, 2], act2.at[past_frames, 6], up)
-    rims2 = [None, take_past_row(act2, outer2[0], 1), low_row]
-    rims2[0] = take_past_row(act2, outer2[1], 4)
     for t in early:
         products(act2, weight2, [(t, r) for r in middle])
     wd_load.wait()

time: 27.9 us -> 27.7 us (level)
  Pallas kernels: 26.2 us -> 25.8 us
    pallas_call x1, Pallas kernels: 26.2 us -> 25.8 us  [per_device(): pl.pallas_call(functools.partial(kernel, GRID_COLUMN_COUNT, grid_rows, gr...]
where the time goes in v6:
time: 27.7 us; the launch traced here: 27.3 us
  Pallas kernels  25.8 us (93%)
  local copies, waits for them, and re-layouts  1.54 us (6%)
    pallas_call x1, Pallas kernels, per_device(): pl.pallas_call(functools.partial(kernel, GRID_COLUMN_COUNT, grid_rows, gr...  25.8 us
    unnamed x1, local copies, waits for them, and re-layouts  1.54 us

profile of v6, /device:TPU:1, one launch (start us, length us, event | category | flops | bytes accessed | tf_op | source)
XLA Modules:
  0.0 27.3 jit_solution(16743459592979524146)
XLA Ops:
  0.0 25.8 %shard_map.109 = bf16[4,96,128]{2,1,0:T(8,128)(2,1)} custom-call(s32[1,4]{1,0:T(1,128)} %links_hbm.1, s32[1,2]{1,0:T(1,128)} %extents_hbm.1, bf16[4,384,128]{2,1,0:T(8,128)(2,1)} %bitcast.7, f32[1,96]{1,0:T(1,128)} %bitcast.9, bf16[96,2592]{1,0:T(8,128)(2,1)} %w1_hbm.1, f32[1,96]{1,0:T(1,128)} %bitcast.10, f32[1,96]{1,0:T(1,128)} %bitcast.11, ...), custom_call_target="tpu_custom_call" | custom-call | tf_op jit(solution)/shard_map/pallas_call | solution.py:657
  25.8 1.5 %copy.13 = bf16[1,4,96,128]{3,2,1,0:T(8,128)(2,1)} copy(bf16[1,4,96,128]{3,2,1,0:T(8,128)(2,1)} %bitcast.8) | data formatting | bytes 196608
